TPU v7x, 512 devices: a whole 4x4x16 slice. The times are simulated.
512 devices in a mesh: row: 64 (over y_hi, z, core), col: 8 (over y_lo, x).
Axes of the slice: x: 4, y: 4 (y_hi: 2, y_lo: 2; y = y_hi * 2 + y_lo), z: 16, core: 2. Of those that a mesh axis runs over, the one named last changes fastest.
Arguments:
- graph_tiles: bfloat16 [512, 8, 19, 128, 128], P('row', 'col'), may hold values from -0.0234375 to 0.0234375
- tile_cols: int32 [512, 8, 19], P('row', 'col'), may hold values from 0 to 511, as said below
- tile_counts: int32 [512, 8], P('row', 'col'), may hold values from 0 to 19, as said below
- pair_order: int32 [256], replicated, may hold values from 0 to 255, as said below
- sketch: bfloat16 [512, 128, 128], P(('row', 'col')), may hold values from -6 to 6
- degree_scale: float32 [512, 128], P(('row', 'col')), may hold values from 0.4 to 2.5
Outputs:
- sketch_basis: float32 [512, 128, 128], P(('row', 'col'))
- core_matrix: float32 [128, 128], replicated
Inputs may be any that keep to these rules, and one draw needn't show every extreme that they name: `pair_order`: a permutation of the pair indices. `tile_counts`: at most 19, the most is reached. `tile_cols`: natural block numbers. For slots s < tile_counts[q, c]: distinct within (q, c), at most the natural block of held row q, and the column's held position h satisfies (h) % 8 = c. Other slots hold arbitrary block numbers and are ignored.
All inputs are finite; a program needn't handle non-finite values.
Results may differ from a plain program's by a relative error of at most 0.0022.
Values may be sent and summed in bfloat16 or wider, within the bound.
No kernel may reach another device: no remote copies, remote signals or barrier semaphores. Data moves between devices by JAX's collectives and lax.ppermute only.
A program may use at most 64 MiB of HBM per device.

v0:
```python
import jax
import jax.numpy as jnp
from jax import lax
from jax.sharding import PartitionSpec as P

EPSILON = 1e-05


def lower_solve(factor, rhs):
    return lax.linalg.triangular_solve(factor, rhs, left_side=True, lower=True)


def held_positions(pair_order):
    pair_count = pair_order.shape[0]
    slot_of = (
        jnp.zeros((pair_count,), jnp.int32)
        .at[pair_order]
        .set(jnp.arange(pair_count, dtype=jnp.int32))
    )
    blocks = jnp.arange(2 * pair_count, dtype=jnp.int32)
    lower_end = jnp.minimum(blocks, 2 * pair_count - 1 - blocks)
    return 2 * slot_of[lower_end] + (blocks >= pair_count).astype(jnp.int32)


def body(graph_tiles, tile_cols, tile_counts, pair_order, sketch, degree_scale):
    slot_count = graph_tiles.shape[2]
    tile_width = graph_tiles.shape[3]
    rank_width = sketch.shape[2]
    shard_blocks = sketch.shape[0]
    row_devices = lax.axis_size("row")
    col_devices = lax.axis_size("col")
    group_blocks = row_devices * shard_blocks
    node_count = 2 * pair_order.shape[0] * tile_width
    held_pos = held_positions(pair_order)
    scaled = (degree_scale[:, :, None] * sketch.astype(jnp.float32)).astype(jnp.bfloat16)
    gathered = lax.all_gather(scaled, "row", axis=0, tiled=True)
    own_rows = lax.all_gather(scaled, "col", axis=0, tiled=True)
    targets = held_pos[tile_cols[:, 0, :]]
    local_index = targets // shard_blocks // col_devices * shard_blocks + targets % shard_blocks
    live_mask = jnp.arange(slot_count, dtype=jnp.int32)[None, :] < tile_counts[:, 0][:, None]
    masked = graph_tiles[:, 0] * live_mask[:, :, None, None].astype(jnp.bfloat16)
    empty_group = jnp.zeros((group_blocks, tile_width, rank_width), jnp.float32)
    operands = jnp.take(gathered, local_index, axis=0)
    forward = jnp.einsum("rsab,rsbk->rak", masked, operands, preferred_element_type=jnp.float32)
    back_terms = jnp.einsum("rsab,rak->rsbk", masked, own_rows, preferred_element_type=jnp.float32)
    partial_value = empty_group.at[local_index.reshape(-1)].add(
        back_terms.reshape(-1, tile_width, rank_width)
    )
    transposed = lax.psum_scatter(partial_value, "row", scatter_dimension=0, tiled=True)
    forward_all = lax.psum(forward, "col")
    own_part = lax.dynamic_slice_in_dim(
        forward_all, lax.axis_index("col") * shard_blocks, shard_blocks, 0
    )
    sketch_image = sketch.astype(jnp.float32) - degree_scale[:, :, None] * (own_part + transposed)
    flat_image = sketch_image.reshape(-1, rank_width)
    flat_sketch = sketch.astype(jnp.float32).reshape(-1, rank_width)
    gram_local = jnp.dot(flat_image.T, flat_image, precision=lax.Precision.HIGHEST)
    cross_local = jnp.dot(flat_sketch.T, flat_image, precision=lax.Precision.HIGHEST)
    gram_total, cross_total = lax.psum((gram_local, cross_local), ("row", "col"))
    gram_sum = gram_total / node_count + EPSILON * jnp.eye(rank_width, dtype=jnp.float32)
    cross_raw = cross_total / node_count
    cross_sum = 0.5 * (cross_raw + cross_raw.T)
    factor = jnp.linalg.cholesky(gram_sum)
    sketch_basis = lower_solve(factor, flat_image.T).T.reshape(shard_blocks, tile_width, rank_width)
    half_way = lower_solve(factor, cross_sum)
    core_matrix = lower_solve(factor, half_way.T)
    return (sketch_basis, core_matrix)


def solution(mesh):
    return jax.shard_map(
        body,
        mesh=mesh,
        in_specs=(
            P("row", "col", None, None, None),
            P("row", "col", None),
            P("row", "col"),
            P(),
            P(("row", "col"), None, None),
            P(("row", "col"), None),
        ),
        out_specs=(P(("row", "col"), None, None), P()),
        check_vma=False,
    )
```

profile of v0, /device:TPU:1, one launch (start us, length us, event | category | flops | bytes accessed | tf_op | source)
XLA Modules:
  0.0 973.9 jit_solution(7340438621631376262)
XLA Ops:
  7.2 1.5 fusion.12
  8.8 0.7 compare_select_fusion.3
  10.2 1.4 scatter_custom_fusion
  11.6 3.5 gather_fusion
  15.2 1.6 gather_fusion.1
  17.1 23.3 %all_gather.7 = bf16[8,128,128]{2,1,0:T(8,128)(2,1)S(1)} all-gather(bf16[1,128,128]{2,1,0:T(8,128)(2,1)S(1)} %copy-done.1), channel_id=1, replica_groups=mesh['row'=64,'col'=8] {'col'}, dimensions={0}, use_global_device_ids=true | all-gather | bytes 294912 | tf_op jit(solution)/shard_map/all_gather | solution.py:37
  40.5 121.0 %all-gather.2.cloned.1.call-done = bf16[64,128,128]{2,1,0:T(8,128)(2,1)} async-done(((bf16[1,128,128]{2,1,0:T(8,128)(2,1)}), bf16[64,128,128]{2,1,0:T(8,128)(2,1)}) %all-gather.2.cloned.1.call-update) | async-done | bytes 2097168 | tf_op jit(solution)/shard_map/all_gather | solution.py:36
  161.5 9.2 gather_fusion.2
  170.7 6.3 fusion.7
  177.1 8.0 fusion.3
  185.1 2.6 broadcast_in_dim.28
  187.7 32.8 %scatter_fusion = f32[64,128,128]{2,1,0:T(8,128)} fusion(f32[64,128,128]{2,1,0:T(8,128)} %broadcast_in_dim.28, s32[152]{0:T(256)S(1)} %bitcast.73, f32[152,128,128]{2,1,0:T(8,128)} %bitcast.69), kind=kCustom, calls=%fused_computation.4 | custom fusion | flops 2490368 | bytes 29885024 | tf_op jit(solution)/shard_map/scatter-add | solution.py:46
  220.8 35.5 %all-reduce.4.cloned.1.call-done = f32[8,128,128]{2,1,0:T(8,128)} async-done(((f32[8,128,128]{2,1,0:T(8,128)}), f32[8,128,128]{2,1,0:T(8,128)}) %all-reduce.4.cloned.1.call-update) | async-done | bytes 524304 | tf_op jit(solution)/shard_map/psum | solution.py:50
  256.3 221.1 %reduce-scatter.2.cloned.1.call-done = f32[1,128,128]{2,1,0:T(8,128)} async-done(((f32[64,128,128]{2,1,0:T(8,128)}), f32[1,128,128]{2,1,0:T(8,128)}) %reduce-scatter.2.cloned.1.call-update) | async-done | bytes 65552 | tf_op jit(solution)/shard_map/reduce_scatter | solution.py:49
  477.4 1.0 convert_subtract_fusion
  478.3 0.9 fusion.22
  479.3 0.9 convolution_bitcast_fusion.1
  480.2 460.0 %all-reduce.6.cloned.1.call-done = (f32[128,128]{0,1:T(8,128)}, f32[128,128]{0,1:T(8,128)}) async-done(((f32[128,128]{0,1:T(8,128)}, f32[128,128]{0,1:T(8,128)}), (f32[128,128]{0,1:T(8,128)}, f32[128,128]{0,1:T(8,128)})) %all-reduce.6.cloned.1.call-update) | async-done | bytes 131088 | tf_op jit(solution)/shard_map/psum | solution.py:59
  940.2 0.9 broadcast_multiply_fusion
  941.3 11.7 %cholesky.19 = f32[128,128]{1,0:T(8,128)S(1)} custom-call(f32[128,128]{1,0:T(8,128)S(1)} %fusion.20), custom_call_target="Cholesky" | custom-call | tf_op jit(solution)/shard_map/jit(cholesky)/cholesky | solution.py:63
  954.4 9.8 %custom-call.8 = f32[1,128,128]{1,2,0:T(8,128)S(1)} custom-call(f32[1,128,128]{2,1,0:T(8,128)S(1)} %fusion.11), custom_call_target="InvertDiagBlocksLowerTriangular" | custom-call | tf_op jit(solution)/shard_map/triangular_solve/custom-call.0 | solution.py:10
  964.5 0.7 copy.25
  965.3 1.1 convolution_bitcast_fusion
  966.4 0.9 fusion.17
  (40 shorter events, 3.5 us)
Async XLA Ops:
  7.2 33.2 %copy-start.3 = (s32[8,1]{0,1:T(1,128)S(1)}, s32[8,1]{0,1:T(1,128)}, u32[]{:S(2)}) copy-start(s32[8,1]{0,1:T(1,128)} %param.10) | copy-start | bytes 100
  7.2 154.3 %all-gather.2.cloned.1.call-start = ((), (), s32[]{:S(2)}) async-start(), calls=%async_computation.1 | async-start | bytes 2129920 | tf_op jit(solution)/shard_map/all_gather | solution.py:36
  8.7 8.4 copy-start.1
  8.7 247.6 %all-reduce.4.cloned.1.call-start = ((), (), s32[]{:S(2)}) async-start(), calls=%async_computation.2 | async-start | bytes 1048576 | tf_op jit(solution)/shard_map/psum | solution.py:50
  177.0 300.3 %reduce-scatter.2.cloned.1.call-start = ((), (), s32[]{:S(2)}) async-start(), calls=%async_computation.3 | async-start | bytes 4259840 | tf_op jit(solution)/shard_map/reduce_scatter | solution.py:49
  187.7 289.7 %copy-start = (bf16[1,128,128]{2,1,0:T(8,128)(2,1)S(1)}, bf16[1,128,128]{2,1,0:T(8,128)(2,1)}, u32[]{:S(2)}) copy-start(bf16[1,128,128]{2,1,0:T(8,128)(2,1)} %param.12) | copy-start | bytes 98308
  187.7 289.7 %copy-start.2 = (f32[1,128]{1,0:T(1,128)S(1)}, f32[1,128]{1,0:T(1,128)}, u32[]{:S(2)}) copy-start(f32[1,128]{1,0:T(1,128)} %param.13) | copy-start | bytes 1540
  220.6 719.6 %all-reduce.6.cloned.1.call-start = ((), (), s32[]{:S(2)}) async-start(), calls=%async_computation.4 | async-start | bytes 262144 | tf_op jit(solution)/shard_map/psum | solution.py:59
Sparse Core Ops, SparseCore 0:
  11.9 149.5 all-gather.1
  177.2 79.1 all-reduce.3
  261.7 215.6 reduce-scatter.1
  483.4 456.7 all-reduce.5
where the time goes:
time: 975 us; the launch traced here: 974 us
  waiting for transfers between devices  838 us (86%)
  other arithmetic  60.5 us (6%)
  blocking collectives  23.3 us (2%)
  local copies, waits for them, and re-layouts  19.6 us (2%)
  matrix products  18.5 us (2%)
  between operations  13.9 us (1%)
    psum x1, waiting for transfers between devices, body(): lax.psum((gram_local, cross_local), ('row', 'col'))  460 us
    reduce_scatter x1, waiting for transfers between devices, body(): lax.psum_scatter(partial_value, 'row', scatter_dimension=0, tiled=True)  221 us
    all_gather x1, waiting for transfers between devices, body(): gathered = lax.all_gather(scaled, 'row', axis=0, tiled=True)  121 us
    psum x1, waiting for transfers between devices, body(): forward_all = lax.psum(forward, 'col')  35.5 us
    scatter-add x1, other arithmetic, body(): empty_group.at[local_index.reshape(-1)]  32.8 us
    all_gather x1, blocking collectives, body(): own_rows = lax.all_gather(scaled, 'col', axis=0, tiled=True)  23.3 us
  transfers between devices with their start and end apart: 4, of which 4 were waited for; matrix products, arithmetic and copies ran while one was open for 5% of the time, Pallas kernels for 0%

commit v1 on v0

v1 whole, which is shorter than its diff:
```python
import jax
import jax.numpy as jnp
from jax import lax
from jax.experimental import pallas as pl
from jax.experimental.pallas import tpu as pltpu
from jax.sharding import Mesh, PartitionSpec as P

EPSILON = 1e-05
AXES = ("yh", "z", "core", "yl", "x")
SIZES = (2, 16, 2, 2, 4)
ROW = ("yh", "z", "core")
COL = ("yl", "x")
PLANE = ("yh", "core", "yl", "x")
GROUP = 4
VMEM_BYTES = 40 * 1024 * 1024
F32 = jnp.float32
BF16 = jnp.bfloat16


def exchange(array, axis):
    return lax.all_to_all(array, axis, 0, 0, tiled=True)


def spread(array, axis):
    count = lax.axis_size(axis)
    return exchange(jnp.broadcast_to(array[None], (count,) + array.shape), axis)


def swap(array, axis):
    return lax.ppermute(array, axis, [(0, 1), (1, 0)])


def full_dot(a, b, contract):
    return lax.dot_general(
        a, b, (contract, ((), ())), precision=lax.Precision.HIGHEST, preferred_element_type=F32
    )


def tile_copy(tiles_hbm, tiles, sems, q):
    return pltpu.make_async_copy(tiles_hbm.at[q, 0], tiles.at[q], sems.at[q])


def transposed_kernel(pos_ref, count_ref, own_ref, tiles_hbm, *rest):
    outs, (tiles, total, tile_sems, out_sems) = rest[:4], rest[4:]
    rows, slots = tiles.shape[0], tiles.shape[1]
    for q in range(rows):
        tile_copy(tiles_hbm, tiles, tile_sems, q).start()
    total[...] = jnp.zeros_like(total)

    def one_row(q, carry):
        tile_copy(tiles_hbm, tiles, tile_sems, q).wait()
        own = own_ref[q]
        count = count_ref[q]
        for first in range(0, slots, GROUP):
            group = range(first, min(first + GROUP, slots))

            @pl.when(count > first)
            def _(group=group):
                places = [pos_ref[q * slots + s] for s in group]
                terms = [
                    jnp.dot(own, tiles[q, s], preferred_element_type=F32) for s in group
                ]
                before = [total[p] for p in places]
                for p, old, term in zip(places, before, terms):
                    total[p] = old + term

        return carry

    lax.fori_loop(0, rows, one_row, 0)
    part = outs[0].shape[0]
    copies = [
        pltpu.make_async_copy(total.at[pl.ds(i * part, part)], out, out_sems.at[i])
        for i, out in enumerate(outs)
    ]
    for copy in copies:
        copy.start()
    for copy in copies:
        copy.wait()


def forward_kernel(pos_ref, count_ref, *rest):
    parts, (tiles_hbm, out_ref, tiles, blocks, total, tile_sems, part_sems) = rest[:4], rest[4:]
    rows, slots = tiles.shape[0], tiles.shape[1]
    part = parts[0].shape[0]
    copies = [
        pltpu.make_async_copy(ref, blocks.at[pl.ds(i * part, part)], part_sems.at[i])
        for i, ref in enumerate(parts)
    ]
    for copy in copies:
        copy.start()
    for q in range(rows):
        tile_copy(tiles_hbm, tiles, tile_sems, q).start()
    blocks[len(parts) * part] = jnp.zeros(blocks.shape[1:], blocks.dtype)
    for copy in copies:
        copy.wait()

    def one_row(q, carry):
        tile_copy(tiles_hbm, tiles, tile_sems, q).wait()
        count = count_ref[q]
        total[...] = jnp.zeros_like(total)
        for first in range(0, slots, GROUP):
            group = range(first, min(first + GROUP, slots))

            @pl.when(count > first)
            def _(group=group):
                left = jnp.concatenate([tiles[q, s] for s in group], axis=1)
                right = jnp.concatenate([blocks[pos_ref[q * slots + s]] for s in group], axis=0)
                total[...] += jnp.dot(left, right, preferred_element_type=F32)

        out_ref[q] = total[...].astype(out_ref.dtype)
        return carry

    lax.fori_loop(0, rows, one_row, 0)


def image_kernel(back_ref, fore_ref, sketch_ref, scale_ref, image_ref, sums_ref):
    back = back_ref[0].astype(F32)
    for i in range(1, back_ref.shape[0]):
        back = back + back_ref[i].astype(F32)
    fore = fore_ref[0].astype(F32)
    for i in range(1, fore_ref.shape[0]):
        fore = fore + fore_ref[i].astype(F32)
    sketch = sketch_ref[...].astype(F32)
    scale = jnp.broadcast_to(scale_ref[...], sketch.shape).T
    image = sketch - scale * (fore + back.T)
    image_ref[...] = image
    width = image.shape[1]
    sums_ref[0:width, :] = full_dot(image, image, ((0,), (0,)))
    sums_ref[width:, :] = full_dot(sketch, image, ((0,), (0,)))


def whiten_kernel(node_count, sums_ref, image_ref, basis_ref, core_ref):
    width = image_ref.shape[1]
    line = lax.broadcasted_iota(jnp.int32, (width, width), 0)
    lane = lax.broadcasted_iota(jnp.int32, (width, width), 1)
    eye = jnp.where(line == lane, 1.0, 0.0).astype(F32)
    gram = sums_ref[0:width, :] / node_count + EPSILON * eye
    cross = sums_ref[width:, :] / node_count
    cross = 0.5 * (cross + cross.T)
    step = 8
    bands = width // step
    left = [gram[step * k : step * (k + 1), :] for k in range(bands)]
    right = [eye[step * k : step * (k + 1), :] for k in range(bands)]
    sub = lax.broadcasted_iota(jnp.int32, (step, width), 0)
    pivots = [jnp.ones((step, width), F32) for _ in range(bands)]
    for j in range(width):
        at, i = divmod(j, step)
        columns = [None] * bands
        for k in range(at, bands):
            columns[k] = jnp.broadcast_to(left[k][:, j : j + 1], (step, width))
        pivot = jnp.broadcast_to(columns[at][i : i + 1, :], (step, width))
        inverse = 1.0 / pivot
        pivots[at] = jnp.where(sub == i, pivot, pivots[at])
        row_left = jnp.broadcast_to(left[at][i : i + 1, :], (step, width)) * inverse
        row_right = jnp.broadcast_to(right[at][i : i + 1, :], (step, width)) * inverse
        columns[at] = jnp.where(sub > i, columns[at], 0.0)
        for k in range(at, bands):
            left[k] = left[k] - columns[k] * row_left
            right[k] = right[k] - columns[k] * row_right
    whitener = jnp.concatenate([r * lax.rsqrt(p) for r, p in zip(right, pivots)], axis=0)
    basis_ref[...] = full_dot(image_ref[...], whitener, ((1,), (1,)))
    half_way = full_dot(whitener, cross, ((1,), (0,)))
    core_ref[...] = full_dot(half_way, whitener, ((1,), (1,)))


def spec(space):
    return pl.BlockSpec(memory_space=space)


def call(kernel, out_shape, in_spaces, out_spaces, scratch, name):
    many = isinstance(out_spaces, tuple)
    return pl.pallas_call(
        kernel,
        out_shape=out_shape,
        in_specs=[spec(s) for s in in_spaces],
        out_specs=tuple(spec(s) for s in out_spaces) if many else spec(out_spaces),
        scratch_shapes=scratch,
        compiler_params=pltpu.CompilerParams(vmem_limit_bytes=VMEM_BYTES),
        name=name,
    )


def body(graph_tiles, tile_cols, tile_counts, pair_order, sketch, degree_scale):
    rows, _, slots, width, _ = graph_tiles.shape
    rank = sketch.shape[2]
    pairs = pair_order.shape[0]
    node_count = 2 * pairs * width
    z_count = lax.axis_size("z")
    col_count = lax.axis_size(COL)
    ANY, VMEM, SMEM = pl.ANY, pltpu.VMEM, pltpu.SMEM

    scaled = (degree_scale[:, :, None] * sketch.astype(F32)).astype(BF16)[0]

    natural = tile_cols[:, 0, :]
    lower_end = jnp.minimum(natural, 2 * pairs - 1 - natural)
    hit = lower_end[:, :, None] == pair_order[None, None, :]
    pair_slot = jnp.sum(jnp.where(hit, jnp.arange(pairs, dtype=jnp.int32), 0), axis=-1)
    held = 2 * pair_slot + (natural >= pairs).astype(jnp.int32)
    owner = held // col_count
    other_core = (owner % 2) ^ lax.axis_index("core")
    other_half = (owner // (2 * z_count)) ^ lax.axis_index("yh")
    place = (other_core * 2 + other_half) * z_count + owner // 2 % z_count
    counts = tile_counts[:, 0]
    live = jnp.arange(slots, dtype=jnp.int32)[None, :] < counts[:, None]
    place = jnp.where(live, place, 4 * z_count).reshape(-1)

    tile_scratch = pltpu.VMEM((rows, slots, width, width), BF16)
    part = jax.ShapeDtypeStruct((z_count, rank, width), F32)

    own_rows = spread(scaled.T, COL)
    keep0, keep1, send0, send1 = call(
        transposed_kernel,
        (part,) * 4,
        (SMEM, SMEM, VMEM, ANY),
        (ANY,) * 4,
        [
            tile_scratch,
            pltpu.VMEM((4 * z_count + 1, rank, width), F32),
            pltpu.SemaphoreType.DMA((rows,)),
            pltpu.SemaphoreType.DMA((4,)),
        ],
        "transposed_products",
    )(place, counts, own_rows, graph_tiles)
    far = (keep1 + swap(send1, "core")).astype(BF16)
    near = swap(send0, "core")
    far = swap(far, "yh")
    scaled, far = lax.optimization_barrier((scaled, far))
    gather0 = lax.all_gather(scaled, "z")
    gather1 = swap(gather0, "yh")
    gather2 = swap(gather0, "core")
    gather3 = swap(gather1, "core")
    back = exchange((keep0 + near + far.astype(F32)).astype(BF16), "z")
    forward = call(
        forward_kernel,
        jax.ShapeDtypeStruct((rows, width, rank), BF16),
        (SMEM, SMEM) + (ANY,) * 5,
        VMEM,
        [
            tile_scratch,
            pltpu.VMEM((4 * z_count + 1, width, rank), BF16),
            pltpu.VMEM((width, rank), F32),
            pltpu.SemaphoreType.DMA((rows,)),
            pltpu.SemaphoreType.DMA((4,)),
        ],
        "forward_products",
    )(place, counts, gather0, gather1, gather2, gather3, graph_tiles)
    fore = exchange(forward, COL)

    image, sums = call(
        image_kernel,
        (jax.ShapeDtypeStruct((width, rank), F32), jax.ShapeDtypeStruct((2 * rank, rank), F32)),
        (VMEM,) * 4,
        (VMEM,) * 2,
        [],
        "image_and_grams",
    )(back, fore, sketch[0], degree_scale)

    pieces = lax.axis_size(PLANE)
    sums = exchange(sums.reshape(pieces, 2 * rank // pieces, rank), PLANE).sum(axis=0)
    sums = spread(sums, "z").sum(axis=0)
    sums = spread(sums, PLANE).reshape(2 * rank, rank)

    def whiten(*refs):
        whiten_kernel(node_count, *refs)

    basis, core_matrix = call(
        whiten,
        (jax.ShapeDtypeStruct((width, rank), F32), jax.ShapeDtypeStruct((rank, rank), F32)),
        (VMEM,) * 2,
        (VMEM,) * 2,
        [],
        "whiten",
    )(sums, image)
    return basis[None], core_matrix


def solution(mesh):
    fine = Mesh(mesh.devices.reshape(SIZES), AXES)
    return jax.shard_map(
        body,
        mesh=fine,
        in_specs=(
            P(ROW, COL, None, None, None),
            P(ROW, COL, None),
            P(ROW, COL),
            P(),
            P(AXES, None, None),
            P(AXES, None),
        ),
        out_specs=(P(AXES, None, None), P()),
        check_vma=False,
    )
```

time: 975 us -> 219 us (0.22)
  waiting for transfers between devices: 838 us -> 25.7 us
  blocking collectives: 23.3 us -> 107 us
  other arithmetic: 60.5 us -> 5.61 us
  starting transfers between devices: 0.34 us -> 41.7 us
  Pallas kernels: 0 us -> 32.7 us
  matrix products: 18.5 us -> 0 us
  local copies, waits for them, and re-layouts: 19.6 us -> 4.38 us
  between operations: 13.9 us -> 0.82 us
    psum x2 -> x0, waiting for transfers between devices: 496 us -> none  [the longest x1 460 us: body(): lax.psum((gram_local, cross_local), ('row', 'col'))]
    reduce_scatter x1 -> x0, waiting for transfers between devices: 221 us -> none  [body(): lax.psum_scatter(partial_value, 'row', scatter_dimension=0, tiled=True)]
    all_gather x1 -> x0, waiting for transfers between devices: 121 us -> none  [body(): gathered = lax.all_gather(scaled, 'row', axis=0, tiled=True)]
    all_to_all x0 -> x4, blocking collectives: none -> 80 us  [exchange(): return lax.all_to_all(array, axis, 0, 0, tiled=True)]
    scatter-add x1 -> x0, other arithmetic: 32.8 us -> none  [body(): empty_group.at[local_index.reshape(-1)]]
    pallas_call x0 -> x4, Pallas kernels: none -> 32.7 us  [the longest x1 18.4 us: body(): call(whiten, (jax.ShapeDtypeStruct((width, rank), F32), jax.ShapeDtypeStr...]
    ppermute x0 -> x6, starting transfers between devices: none -> 32.5 us  [swap(): return lax.ppermute(array, axis, [(0, 1), (1, 0)])]
    another operation x5 -> x0, other arithmetic: 22.9 us -> none  [the longest x3 12.4 us: body(): factor = jnp.linalg.cholesky(gram_sum)]
  transfers between devices with their start and end apart: 4 -> 8, of which waited for: 4 -> 5; matrix products, arithmetic and copies ran while one was open for 5% -> 2% of each run, Pallas kernels for 0% -> 3%
where the time goes in v1:
time: 219 us; the launch traced here: 218 us
  blocking collectives  107 us (49%)
  starting transfers between devices  41.7 us (19%)
  Pallas kernels  32.7 us (15%)
  waiting for transfers between devices  25.7 us (12%)
  other arithmetic  5.61 us (3%)
  local copies, waits for them, and re-layouts  4.38 us (2%)
    all_to_all x4, blocking collectives, exchange(): return lax.all_to_all(array, axis, 0, 0, tiled=True)  80 us
    ppermute x6, starting transfers between devices, swap(): return lax.ppermute(array, axis, [(0, 1), (1, 0)])  32.5 us
    all_gather x1, blocking collectives, body(): gather0 = lax.all_gather(scaled, 'z')  27.2 us
    pallas_call x1, Pallas kernels, body(): call(whiten, (jax.ShapeDtypeStruct((width, rank), F32), jax.ShapeDtypeStr...  18.4 us
    ppermute x6, waiting for transfers between devices, swap(): return lax.ppermute(array, axis, [(0, 1), (1, 0)])  18.4 us
    all_to_all x2, starting transfers between devices, exchange(): return lax.all_to_all(array, axis, 0, 0, tiled=True)  9.28 us
    all_to_all x2, waiting for transfers between devices, exchange(): return lax.all_to_all(array, axis, 0, 0, tiled=True)  7.32 us
    pallas_call x1, Pallas kernels, body(): call(forward_kernel, jax.ShapeDtypeStruct((rows, width, rank), BF16), (SM...  7.07 us
  transfers between devices with their start and end apart: 8, of which 5 were waited for; matrix products, arithmetic and copies ran while one was open for 2% of the time, Pallas kernels for 3%

profile of v1, /device:TPU:1, one launch (start us, length us, event | category | flops | bytes accessed | tf_op | source)
XLA Modules:
  0.0 218.1 jit_solution(6469357284279310118)
XLA Ops:
  2.4 5.9 %all-to-all-start = ((bf16[8,128,128]{2,1,0:T(8,128)(2,1)}), bf16[8,128,128]{2,1,0:T(8,128)(2,1)S(1)}, u32[]{:S(2)}, u32[]{:S(2)}) async-start(bf16[8,128,128]{2,1,0:T(8,128)(2,1)} %broadcast_in_dim.40), calls=%async_computation | async-start | bytes 524288 | tf_op jit(solution)/shard_map/all_to_all | solution.py:21
  9.7 1.2 select_reduce_fusion
  12.0 2.4 %all-to-all-done.own_ref = bf16[8,128,128]{2,1,0:T(8,128)(2,1)S(1)} async-done(((bf16[8,128,128]{2,1,0:T(8,128)(2,1)}), bf16[8,128,128]{2,1,0:T(8,128)(2,1)S(1)}, u32[]{:S(2)}, u32[]{:S(2)}) %all-to-all-start) | async-done | bytes 262176 | tf_op jit(solution)/shard_map/all_to_all | solution.py:21
  14.4 2.4 %copy-done = bf16[8,1,19,128,128]{4,3,2,1,0:T(8,128)(2,1)S(1)} copy-done((bf16[8,1,19,128,128]{4,3,2,1,0:T(8,128)(2,1)S(1)}, bf16[8,1,19,128,128]{4,3,2,1,0:T(8,128)(2,1)}, u32[]{:S(2)}) %copy-start) | copy-done | bytes 4980760
  17.4 6.8 %transposed_products.1 = (f32[16,128,128]{2,1,0:T(8,128)S(1)}, f32[16,128,128]{2,1,0:T(8,128)S(1)}, f32[16,128,128]{2,1,0:T(8,128)S(1)}, f32[16,128,128]{2,1,0:T(8,128)S(1)}) custom-call(s32[152]{0:T(256)S(1)} %fusion.6.pos_ref, s32[8]{0:T(128)S(1)} %bitcast.20, bf16[8,128,128]{2,1,0:T(8,128)(2,1)S(1)} %all-to-all-done.own_ref, ...), custom_call_target="tpu_custom_call" | custom-call | tf_op jit(solution)/shard_map/transposed_products/pallas_call | solution.py:211
  24.3 8.0 %collective-permute-start.1 = (f32[16,128,128]{2,1,0:T(8,128)S(1)}, f32[16,128,128]{2,1,0:T(8,128)S(1)}, u32[]{:S(2)}, u32[]{:S(2)}) collective-permute-start(f32[16,128,128]{2,1,0:T(8,128)S(1)} %get-tuple-element.15), channel_id=1, source_target_pairs={{0,8},{8,0},{1,9},{9,1},{2,10},{10,2},{3,11},{11,3},{4,12},{12,4},... | collective-permute-start | bytes 3145736 | tf_op jit(solution)/shard_map/ppermute | solution.py:30
  32.2 2.3 %collective-permute-done.1 = f32[16,128,128]{2,1,0:T(8,128)S(1)} collective-permute-done((f32[16,128,128]{2,1,0:T(8,128)S(1)}, f32[16,128,128]{2,1,0:T(8,128)S(1)}, u32[]{:S(2)}, u32[]{:S(2)}) %collective-permute-start.1) | collective-permute-done | bytes 1048608 | tf_op jit(solution)/shard_map/ppermute | solution.py:30
  34.6 1.9 collective-permute-start.2
  36.5 14.6 %collective-permute-done.2 = bf16[16,128,128]{2,1,0:T(8,128)(2,1)S(1)} collective-permute-done((bf16[16,128,128]{2,1,0:T(8,128)(2,1)S(1)}, bf16[16,128,128]{2,1,0:T(8,128)(2,1)S(1)}, u32[]{:S(2)}, u32[]{:S(2)}) %collective-permute-start.2) | collective-permute-done | bytes 524320 | tf_op jit(solution)/shard_map/ppermute | solution.py:30
  51.2 27.2 %all-gather = bf16[2048,128]{1,0:T(8,128)(2,1)S(1)} all-gather(bf16[128,128]{1,0:T(8,128)(2,1)S(1)} %get-tuple-element.17), channel_id=2, replica_groups=mesh['yh'=2,'z'=16,'core'=2,'yl'=2,'x'=4] {'z'}, dimensions={0}, use_global_device_ids=true | all-gather | bytes 557056 | tf_op jit(solution)/shard_map/all_gather | solution.py:228
  78.4 5.6 %collective-permute-start.3 = (bf16[16,128,128]{2,1,0:T(8,128)(2,1)S(1)}, bf16[16,128,128]{2,1,0:T(8,128)(2,1)S(1)}, u32[]{:S(2)}, u32[]{:S(2)}) collective-permute-start(bf16[16,128,128]{2,1,0:T(8,128)(2,1)S(1)} %bitcast.13), channel_id=1, source_target_pairs={{0,256},{256,0},{1,257},{257,1},{2,258},{258,2},{3,259},{259,3},{4... | collective-permute-start | bytes 1572872 | tf_op jit(solution)/shard_map/ppermute | solution.py:30
  84.0 9.7 %collective-permute-start = (f32[16,128,128]{2,1,0:T(8,128)S(1)}, f32[16,128,128]{2,1,0:T(8,128)S(1)}, u32[]{:S(2)}, u32[]{:S(2)}) collective-permute-start(f32[16,128,128]{2,1,0:T(8,128)S(1)} %get-tuple-element.13), channel_id=1, source_target_pairs={{0,8},{8,0},{1,9},{9,1},{2,10},{10,2},{3,11},{11,3},{4,12},{12,4},... | collective-permute-start | bytes 3145736 | tf_op jit(solution)/shard_map/ppermute | solution.py:30
  93.7 1.9 collective-permute-start.4
  95.7 5.4 %collective-permute-start.5 = (bf16[16,128,128]{2,1,0:T(8,128)(2,1)S(1)}, bf16[16,128,128]{2,1,0:T(8,128)(2,1)S(1)}, u32[]{:S(2)}, u32[]{:S(2)}) collective-permute-start(bf16[16,128,128]{2,1,0:T(8,128)(2,1)S(1)} %collective-permute-done.3.rest_1_), channel_id=1, source_target_pairs={{0,8},{8,0},{1,9},{9,1},{2,10},{10,2},{3,11},{11,3},{4,12},{12,4},... | collective-permute-start | bytes 1572872 | tf_op jit(solution)/shard_map/ppermute | solution.py:30
  101.1 1.5 collective-permute-done.5.rest_3_
  102.6 7.1 %forward_products.1 = bf16[8,128,128]{2,1,0:T(8,128)(2,1)} custom-call(s32[152]{0:T(256)S(1)} %fusion.6.pos_ref, s32[8]{0:T(128)S(1)} %bitcast.21, bf16[16,128,128]{2,1,0:T(8,128)(2,1)S(1)} %bitcast.15, bf16[16,128,128]{2,1,0:T(8,128)(2,1)S(1)} %collective-permute-done.3.rest_1_, bf16[16,128,128]{2,1,0:T(8,128)(2,1)S(1)} %collective-permute-done.4.rest_2_, ...), custom_call_target="tpu_custom_call" | custom-call | tf_op jit(solution)/shard_map/forward_products/pallas_call | solution.py:233
  109.6 3.4 %all-to-all-start.2 = ((bf16[8,128,128]{2,1,0:T(8,128)(2,1)}), bf16[8,128,128]{2,1,0:T(8,128)(2,1)S(1)}, u32[]{:S(2)}, u32[]{:S(2)}) async-start(bf16[8,128,128]{2,1,0:T(8,128)(2,1)} %forward_products.1), calls=%async_computation.2 | async-start | bytes 524288 | tf_op jit(solution)/shard_map/all_to_all | solution.py:21
  113.1 1.3 add_convert_fusion
  114.3 4.9 %all-to-all-done.2.fore_ref = bf16[8,128,128]{2,1,0:T(8,128)(2,1)S(1)} async-done(((bf16[8,128,128]{2,1,0:T(8,128)(2,1)}), bf16[8,128,128]{2,1,0:T(8,128)(2,1)S(1)}, u32[]{:S(2)}, u32[]{:S(2)}) %all-to-all-start.2) | async-done | bytes 262176 | tf_op jit(solution)/shard_map/all_to_all | solution.py:21
  119.3 31.0 %all_to_all.30.back_ref = bf16[16,128,128]{2,1,0:T(8,128)(2,1)S(1)} all-to-all(bf16[16,128,128]{2,1,0:T(8,128)(2,1)S(1)} %add_convert_fusion), channel_id=1, replica_groups=mesh['yh'=2,'z'=16,'core'=2,'yl'=2,'x'=4] {'z'}, dimensions={0} | all-to-all | bytes 1048576 | tf_op jit(solution)/shard_map/all_to_all | solution.py:21
  150.7 17.9 %all_to_all.31 = f32[32,8,128]{2,1,0:T(8,128)S(1)} all-to-all(f32[32,8,128]{2,1,0:T(8,128)S(1)} %bitcast.18), channel_id=1, replica_groups=mesh['yh'=2,'z'=16,'core'=2,'yl'=2,'x'=4] {'yh','core','yl','x'}, dimensions={0} | all-to-all | bytes 262144 | tf_op jit(solution)/shard_map/all_to_all | solution.py:21
  168.6 18.1 %all_to_all.32 = f32[16,8,128]{2,1,0:T(8,128)S(1)} all-to-all(f32[16,8,128]{2,1,0:T(8,128)S(1)} %broadcast_in_dim.41), channel_id=1, replica_groups=mesh['yh'=2,'z'=16,'core'=2,'yl'=2,'x'=4] {'z'}, dimensions={0} | all-to-all | bytes 131072 | tf_op jit(solution)/shard_map/all_to_all | solution.py:21
  186.7 13.0 %all_to_all.33 = f32[32,8,128]{2,1,0:T(8,128)S(1)} all-to-all(f32[32,8,128]{2,1,0:T(8,128)S(1)} %broadcast_in_dim.42), channel_id=1, replica_groups=mesh['yh'=2,'z'=16,'core'=2,'yl'=2,'x'=4] {'yh','core','yl','x'}, dimensions={0} | all-to-all | bytes 262144 | tf_op jit(solution)/shard_map/all_to_all | solution.py:21
  199.8 18.4 %whiten.1 = (f32[128,128]{1,0:T(8,128)}, f32[128,128]{1,0:T(8,128)}) custom-call(f32[256,128]{1,0:T(8,128)S(1)} %bitcast.16, f32[128,128]{1,0:T(8,128)S(1)} %get-tuple-element.19.refs_1_), custom_call_target="tpu_custom_call" | custom-call | tf_op jit(solution)/shard_map/whiten/pallas_call | solution.py:266
  (35 shorter events, 5.6 us)
Async XLA Ops:
  0.6 101.9 %copy-start.4 = (s32[8,1]{0,1:T(1,128)S(1)}, s32[8,1]{0,1:T(1,128)}, u32[]{:S(2)}) copy-start(s32[8,1]{0,1:T(1,128)} %param.8) | copy-start | bytes 100
  2.4 12.0 %all-to-all-start = ((bf16[8,128,128]{2,1,0:T(8,128)(2,1)}), bf16[8,128,128]{2,1,0:T(8,128)(2,1)S(1)}, u32[]{:S(2)}, u32[]{:S(2)}) async-start(bf16[8,128,128]{2,1,0:T(8,128)(2,1)} %broadcast_in_dim.40), calls=%async_computation | async-start | bytes 524288 | tf_op jit(solution)/shard_map/all_to_all | solution.py:21
  14.4 2.4 %copy-start = (bf16[8,1,19,128,128]{4,3,2,1,0:T(8,128)(2,1)S(1)}, bf16[8,1,19,128,128]{4,3,2,1,0:T(8,128)(2,1)}, u32[]{:S(2)}) copy-start(bf16[8,1,19,128,128]{4,3,2,1,0:T(8,128)(2,1)} %rest_4_.1) | copy-start | bytes 14942212
  16.8 0.7 copy-start.3
  17.4 85.1 %copy-start.1 = (bf16[8,1,19,128,128]{4,3,2,1,0:T(8,128)(2,1)S(1)}, bf16[8,1,19,128,128]{4,3,2,1,0:T(8,128)(2,1)}, u32[]{:S(2)}) copy-start(bf16[8,1,19,128,128]{4,3,2,1,0:T(8,128)(2,1)} %rest_4_.1) | copy-start | bytes 14942212
  24.3 10.2 %collective-permute-start.1 = (f32[16,128,128]{2,1,0:T(8,128)S(1)}, f32[16,128,128]{2,1,0:T(8,128)S(1)}, u32[]{:S(2)}, u32[]{:S(2)}) collective-permute-start(f32[16,128,128]{2,1,0:T(8,128)S(1)} %get-tuple-element.15), channel_id=1, source_target_pairs={{0,8},{8,0},{1,9},{9,1},{2,10},{10,2},{3,11},{11,3},{4,12},{12,4},... | collective-permute-start | bytes 3145736 | tf_op jit(solution)/shard_map/ppermute | solution.py:30
  34.6 16.5 %collective-permute-start.2 = (bf16[16,128,128]{2,1,0:T(8,128)(2,1)S(1)}, bf16[16,128,128]{2,1,0:T(8,128)(2,1)S(1)}, u32[]{:S(2)}, u32[]{:S(2)}) collective-permute-start(bf16[16,128,128]{2,1,0:T(8,128)(2,1)S(1)} %add_convert_fusion.1), channel_id=1, source_target_pairs={{0,256},{256,0},{1,257},{257,1},{2,258},{258,2},{3,259},{259,3},{4... | collective-permute-start | bytes 1572872 | tf_op jit(solution)/shard_map/ppermute | solution.py:30
  51.2 49.9 %copy-start.6 = (bf16[16,128,128]{2,1,0:T(8,128)(2,1)}, bf16[16,128,128]{2,1,0:T(8,128)(2,1)S(1)}, u32[]{:S(2)}) copy-start(bf16[16,128,128]{2,1,0:T(8,128)(2,1)S(1)} %collective-permute-done.2) | copy-start | bytes 1572868
  78.4 17.3 %collective-permute-start.3 = (bf16[16,128,128]{2,1,0:T(8,128)(2,1)S(1)}, bf16[16,128,128]{2,1,0:T(8,128)(2,1)S(1)}, u32[]{:S(2)}, u32[]{:S(2)}) collective-permute-start(bf16[16,128,128]{2,1,0:T(8,128)(2,1)S(1)} %bitcast.13), channel_id=1, source_target_pairs={{0,256},{256,0},{1,257},{257,1},{2,258},{258,2},{3,259},{259,3},{4... | collective-permute-start | bytes 1572872 | tf_op jit(solution)/shard_map/ppermute | solution.py:30
  84.0 66.3 %copy-start.2 = (bf16[1,128,128]{2,1,0:T(8,128)(2,1)S(1)}, bf16[1,128,128]{2,1,0:T(8,128)(2,1)}, u32[]{:S(2)}) copy-start(bf16[1,128,128]{2,1,0:T(8,128)(2,1)} %param.10) | copy-start | bytes 98308
  84.0 66.3 %copy-start.5 = (f32[1,128]{1,0:T(1,128)S(1)}, f32[1,128]{1,0:T(1,128)}, u32[]{:S(2)}) copy-start(f32[1,128]{1,0:T(1,128)} %scale_ref.1) | copy-start | bytes 1540
  84.0 29.1 %collective-permute-start = (f32[16,128,128]{2,1,0:T(8,128)S(1)}, f32[16,128,128]{2,1,0:T(8,128)S(1)}, u32[]{:S(2)}, u32[]{:S(2)}) collective-permute-start(f32[16,128,128]{2,1,0:T(8,128)S(1)} %get-tuple-element.13), channel_id=1, source_target_pairs={{0,8},{8,0},{1,9},{9,1},{2,10},{10,2},{3,11},{11,3},{4,12},{12,4},... | collective-permute-start | bytes 3145736 | tf_op jit(solution)/shard_map/ppermute | solution.py:30
  93.7 7.3 %collective-permute-start.4 = (bf16[16,128,128]{2,1,0:T(8,128)(2,1)S(1)}, bf16[16,128,128]{2,1,0:T(8,128)(2,1)S(1)}, u32[]{:S(2)}, u32[]{:S(2)}) collective-permute-start(bf16[16,128,128]{2,1,0:T(8,128)(2,1)S(1)} %bitcast.14), channel_id=1, source_target_pairs={{0,8},{8,0},{1,9},{9,1},{2,10},{10,2},{3,11},{11,3},{4,12},{12,4},... | collective-permute-start | bytes 1572872 | tf_op jit(solution)/shard_map/ppermute | solution.py:30
  95.7 6.9 %collective-permute-start.5 = (bf16[16,128,128]{2,1,0:T(8,128)(2,1)S(1)}, bf16[16,128,128]{2,1,0:T(8,128)(2,1)S(1)}, u32[]{:S(2)}, u32[]{:S(2)}) collective-permute-start(bf16[16,128,128]{2,1,0:T(8,128)(2,1)S(1)} %collective-permute-done.3.rest_1_), channel_id=1, source_target_pairs={{0,8},{8,0},{1,9},{9,1},{2,10},{10,2},{3,11},{11,3},{4,12},{12,4},... | collective-permute-start | bytes 1572872 | tf_op jit(solution)/shard_map/ppermute | solution.py:30
  109.6 9.6 %all-to-all-start.2 = ((bf16[8,128,128]{2,1,0:T(8,128)(2,1)}), bf16[8,128,128]{2,1,0:T(8,128)(2,1)S(1)}, u32[]{:S(2)}, u32[]{:S(2)}) async-start(bf16[8,128,128]{2,1,0:T(8,128)(2,1)} %forward_products.1), calls=%async_computation.2 | async-start | bytes 524288 | tf_op jit(solution)/shard_map/all_to_all | solution.py:21

commit v2 on v1

v2 whole, which is shorter than its diff:
```python
import jax
import jax.numpy as jnp
from jax import lax
from jax.experimental import pallas as pl
from jax.experimental.pallas import tpu as pltpu
from jax.sharding import Mesh, PartitionSpec as P

EPSILON = 1e-05
AXES = ("yh", "z", "core", "yl", "x")
SIZES = (2, 16, 2, 2, 4)
ROW = ("yh", "z", "core")
COL = ("yl", "x")
PLANE = ("yh", "core", "yl", "x")
GROUP = 19
NO_COST = pl.CostEstimate(flops=0, bytes_accessed=0, transcendentals=0)
VMEM_BYTES = 57 * 1024 * 1024
F32 = jnp.float32
BF16 = jnp.bfloat16


def exchange(array, axis):
    return lax.all_to_all(array, axis, 0, 0, tiled=True)


def spread(array, axis):
    return exchange(jnp.broadcast_to(array[None], (lax.axis_size(axis),) + array.shape), axis)


def swap(array, axis):
    return lax.ppermute(array, axis, [(0, 1), (1, 0)])


def after(array, *others):
    return lax.optimization_barrier((array, *others))[0]


def full_dot(a, b, contract):
    return lax.dot_general(
        a, b, (contract, ((), ())), precision=lax.Precision.HIGHEST, preferred_element_type=F32
    )


def tile_copy(tiles_hbm, tiles, sems, q):
    return pltpu.make_async_copy(tiles_hbm.at[q, 0], tiles.at[q], sems.at[q])


def place_kernel(order_ref, cols_ref, count_ref, place_ref, slot_of):
    rows, slots = cols_ref.shape
    pairs = order_ref.shape[0]
    core, half = lax.axis_index("core"), lax.axis_index("yh")

    def one_pair(p, carry):
        slot_of[order_ref[p]] = p
        return carry

    lax.fori_loop(0, pairs, one_pair, 0, unroll=16)

    def one_row(q, carry):
        count = count_ref[q, 0]
        for s in range(slots):
            natural = cols_ref[q, s]
            upper = natural >= pairs
            slot = slot_of[jnp.where(upper, 2 * pairs - 1 - natural, natural)]
            owner = lax.shift_right_logical(2 * slot + upper.astype(jnp.int32), 3)
            side = 2 * ((owner & 1) ^ core) + ((lax.shift_right_logical(owner, 5) & 1) ^ half)
            place = side * 16 + (lax.shift_right_logical(owner, 1) & 15)
            place_ref[q * slots + s] = jnp.where(s < count, place, 64)
        return carry

    lax.fori_loop(0, rows, one_row, 0)


def scale_kernel(sketch_ref, scale_ref, own_ref, gather_ref):
    sketch = sketch_ref[...].astype(F32)
    scaled = jnp.broadcast_to(scale_ref[...], sketch.shape).T * sketch
    turned, scaled = scaled.T.astype(BF16), scaled.astype(BF16)
    for i in range(own_ref.shape[0]):
        own_ref[i] = turned
    for i in range(gather_ref.shape[0]):
        gather_ref[i] = scaled


def transposed_kernel(pos_ref, count_ref, own_hbm, tiles_hbm, *rest):
    outs, (own_ref, tiles, total, own_sem, tile_sems, out_sems) = rest[:4], rest[4:]
    rows, slots = tiles.shape[0], tiles.shape[1]
    z_count = outs[0].shape[0]
    own_copy = pltpu.make_async_copy(own_hbm, own_ref, own_sem)
    own_copy.start()
    for q in range(rows):
        tile_copy(tiles_hbm, tiles, tile_sems, q).start()
    total[...] = jnp.zeros_like(total)
    own_copy.wait()

    def one_row(q, carry):
        tile_copy(tiles_hbm, tiles, tile_sems, q).wait()
        own = own_ref[q]
        count = count_ref[q, 0]
        for first in range(0, slots, GROUP):
            group = range(first, min(first + GROUP, slots))

            @pl.when(count > first)
            def _(group=group):
                places = [pos_ref[q * slots + s] for s in group]
                terms = [jnp.dot(own, tiles[q, s], preferred_element_type=F32) for s in group]
                before = [total[p] for p in places]
                for p, old, term in zip(places, before, terms):
                    total[p] = old + term

        return carry

    lax.fori_loop(0, rows, one_row, 0)
    copies = [
        pltpu.make_async_copy(total.at[pl.ds(i * z_count, z_count)], out, out_sems.at[i])
        for i, out in enumerate(outs)
    ]
    for copy in copies:
        copy.start()
    for copy in copies:
        copy.wait()


def forward_kernel(pos_ref, count_ref, *rest):
    parts, (tiles_hbm, out_ref, tiles, blocks, total, tile_sems, part_sems) = rest[:4], rest[4:]
    rows, slots = tiles.shape[0], tiles.shape[1]
    part = parts[0].shape[0]
    copies = [
        pltpu.make_async_copy(ref, blocks.at[pl.ds(i * part, part)], part_sems.at[i])
        for i, ref in enumerate(parts)
    ]
    for copy in copies:
        copy.start()
    ahead = 3
    for q in range(ahead):
        tile_copy(tiles_hbm, tiles, tile_sems, q).start()
    blocks[4 * part] = jnp.zeros(blocks.shape[1:], blocks.dtype)
    for copy in copies:
        copy.wait()

    def one_row(q, carry):
        tile_copy(tiles_hbm, tiles, tile_sems, q).wait()

        @pl.when(q + ahead < rows)
        def _():
            tile_copy(tiles_hbm, tiles, tile_sems, q + ahead).start()

        count = count_ref[q, 0]
        total[...] = jnp.zeros_like(total)
        for first in range(0, slots, GROUP):
            group = range(first, min(first + GROUP, slots))

            @pl.when(count > first)
            def _(group=group):
                left = jnp.concatenate([tiles[q, s] for s in group], axis=1)
                right = jnp.concatenate([blocks[pos_ref[q * slots + s]] for s in group], axis=0)
                total[...] += jnp.dot(left, right, preferred_element_type=F32)

        out_ref[q] = total[...].astype(out_ref.dtype)
        return carry

    lax.fori_loop(0, rows, one_row, 0)


def image_kernel(back_ref, fore_ref, sketch_ref, scale_ref, image_ref, sums_ref):
    back = back_ref[...]
    fore = fore_ref[0].astype(F32)
    for i in range(1, fore_ref.shape[0]):
        fore = fore + fore_ref[i].astype(F32)
    sketch = sketch_ref[...].astype(F32)
    scale = jnp.broadcast_to(scale_ref[...], sketch.shape).T
    image = sketch - scale * (fore + back.T)
    image_ref[...] = image
    width = image.shape[1]
    sums_ref[0:width, :] = full_dot(image, image, ((0,), (0,)))
    sums_ref[width:, :] = full_dot(sketch, image, ((0,), (0,)))


def whiten_kernel(node_count, sums_ref, image_ref, basis_ref, core_ref):
    width = image_ref.shape[1]
    line = lax.broadcasted_iota(jnp.int32, (width, width), 0)
    lane = lax.broadcasted_iota(jnp.int32, (width, width), 1)
    eye = jnp.where(line == lane, 1.0, 0.0).astype(F32)
    gram = sums_ref[0:width, :] / node_count + EPSILON * eye
    cross = sums_ref[width:, :] / node_count
    cross = 0.5 * (cross + cross.T)
    step = 8
    bands = width // step
    left = [gram[step * k : step * (k + 1), :] for k in range(bands)]
    right = [eye[step * k : step * (k + 1), :] for k in range(bands)]
    sub = lax.broadcasted_iota(jnp.int32, (step, width), 0)

    def line_of(band, i):
        return jnp.broadcast_to(band[i : i + 1, :], (step, width))

    def lane_of(band, j):
        return jnp.broadcast_to(band[:, j : j + 1], (step, width))

    whitener = []
    for at in range(bands):
        first = step * at
        lanes = [lane_of(left[at], first + i) for i in range(step)]
        block = [[line_of(lanes[j], i) for j in range(i + 1)] for i in range(step)]
        lower = [[None] * step for _ in range(step)]
        inverse = []
        for j in range(step):
            inverse.append(1.0 / block[j][j])
            for i in range(j + 1, step):
                lower[i][j] = block[i][j] * inverse[j]
            for i in range(j + 1, step):
                for k in range(j + 1, i + 1):
                    block[i][k] = block[i][k] - lower[i][j] * block[k][j]
        solved = []
        for band in (left[at], right[at]):
            lines = [line_of(band, i) for i in range(step)]
            for j in range(step):
                for i in range(j + 1, step):
                    lines[i] = lines[i] - lower[i][j] * lines[j]
            solved.append(lines)
        scaled = jnp.zeros((step, width), F32)
        for i in range(step):
            scaled = jnp.where(sub == i, solved[1][i] * lax.rsqrt(block[i][i]), scaled)
        whitener.append(scaled)
        if at + 1 == bands:
            break
        for lines in solved:
            for i in range(step):
                lines[i] = lines[i] * inverse[i]
            for j in reversed(range(step)):
                for i in range(j):
                    lines[i] = lines[i] - lower[j][i] * lines[j]
        for k in range(at + 1, bands):
            lanes = [lane_of(left[k], first + i) for i in range(step)]
            for i in range(step):
                left[k] = left[k] - lanes[i] * solved[0][i]
                right[k] = right[k] - lanes[i] * solved[1][i]
    whitener = jnp.concatenate(whitener, axis=0)
    basis_ref[...] = full_dot(image_ref[...], whitener, ((1,), (1,)))
    half_way = full_dot(whitener, cross, ((1,), (0,)))
    core_ref[...] = full_dot(half_way, whitener, ((1,), (1,)))


def spec(space):
    return pl.BlockSpec(memory_space=space)


def call(kernel, out_shape, in_spaces, out_spaces, scratch, name, cost=NO_COST):
    many = isinstance(out_spaces, tuple)
    return pl.pallas_call(
        kernel,
        out_shape=out_shape,
        in_specs=[spec(s) for s in in_spaces],
        out_specs=tuple(spec(s) for s in out_spaces) if many else spec(out_spaces),
        scratch_shapes=scratch,
        compiler_params=pltpu.CompilerParams(vmem_limit_bytes=VMEM_BYTES),
        cost_estimate=cost,
        name=name,
    )


def body(graph_tiles, tile_cols, tile_counts, pair_order, sketch, degree_scale):
    rows, _, slots, width, _ = graph_tiles.shape
    rank = sketch.shape[2]
    pairs = pair_order.shape[0]
    node_count = 2 * pairs * width
    z_count = lax.axis_size("z")
    HBM, VMEM, SMEM = pltpu.HBM, pltpu.VMEM, pltpu.SMEM

    own_rows, gather = call(
        scale_kernel,
        (
            jax.ShapeDtypeStruct((lax.axis_size(COL), rank, width), BF16),
            jax.ShapeDtypeStruct((z_count, width, rank), BF16),
        ),
        (VMEM,) * 2,
        (VMEM,) * 2,
        [],
        "scale",
    )(sketch[0], degree_scale)
    tile_scratch = pltpu.VMEM((rows, slots, width, width), BF16)
    row_sems = pltpu.SemaphoreType.DMA((rows,))
    part_sems = pltpu.SemaphoreType.DMA((4,))
    part = jax.ShapeDtypeStruct((z_count, rank, width), F32)

    places = call(
        place_kernel,
        jax.ShapeDtypeStruct((rows * slots,), jnp.int32),
        (SMEM, SMEM, SMEM),
        SMEM,
        [pltpu.SMEM((pairs,), jnp.int32)],
        "places",
    )(pair_order, tile_cols[:, 0, :], tile_counts)
    own_rows = exchange(own_rows, COL)
    gather = exchange(after(gather, places), "z")
    near, far, near_send, far_send = call(
        transposed_kernel,
        (part,) * 4,
        (SMEM, SMEM, HBM, HBM),
        (HBM,) * 4,
        [
            pltpu.VMEM((rows, rank, width), BF16),
            tile_scratch,
            pltpu.VMEM((4 * z_count + 1, rank, width), F32),
            pltpu.SemaphoreType.DMA,
            row_sems,
            part_sems,
        ],
        "transposed_products",
    )(places, tile_counts, own_rows, graph_tiles)
    far_got = swap(far_send, "core")
    near_got = swap(near_send, "core")
    far = (far + far_got).astype(BF16)
    near = lax.optimization_barrier(near + near_got)
    back = (near + swap(far, "yh").astype(F32)).astype(BF16)
    gather = after(gather, far, near_got)
    gather1 = after(swap(gather, "yh"), back)
    gather2 = swap(gather, "core")
    gather3 = swap(gather1, "core")
    back = exchange(back, "z")
    forward = call(
        forward_kernel,
        jax.ShapeDtypeStruct((rows, width, rank), BF16),
        (SMEM, SMEM) + (HBM,) * 5,
        VMEM,
        [
            tile_scratch,
            pltpu.VMEM((4 * z_count + 1, width, rank), BF16),
            pltpu.VMEM((width, rank), F32),
            row_sems,
            part_sems,
        ],
        "forward_products",
        pl.CostEstimate(flops=12650000000, bytes_accessed=0, transcendentals=0),
    )(places, tile_counts, gather, gather1, gather2, gather3, graph_tiles)
    fore = exchange(after(forward, back), COL)
    back = back.astype(F32).sum(axis=0)

    image, sums = call(
        image_kernel,
        (jax.ShapeDtypeStruct((width, rank), F32), jax.ShapeDtypeStruct((2 * rank, rank), F32)),
        (VMEM,) * 4,
        (VMEM,) * 2,
        [],
        "image_and_grams",
    )(back, fore, sketch[0], degree_scale)

    pieces = lax.axis_size(PLANE)
    sums = exchange(sums.reshape(pieces, 2 * rank // pieces, rank), PLANE).sum(axis=0)
    sums = spread(sums, "z").sum(axis=0)
    sums = spread(sums, PLANE).reshape(2 * rank, rank)

    def whiten(*refs):
        whiten_kernel(node_count, *refs)

    basis, core_matrix = call(
        whiten,
        (jax.ShapeDtypeStruct((width, rank), F32), jax.ShapeDtypeStruct((rank, rank), F32)),
        (VMEM,) * 2,
        (VMEM,) * 2,
        [],
        "whiten",
    )(sums, image)
    return basis[None], core_matrix


def solution(mesh):
    fine = Mesh(mesh.devices.reshape(SIZES), AXES)
    return jax.shard_map(
        body,
        mesh=fine,
        in_specs=(
            P(ROW, COL, None, None, None),
            P(ROW, COL, None),
            P(ROW, COL),
            P(),
            P(AXES, None, None),
            P(AXES, None),
        ),
        out_specs=(P(AXES, None, None), P()),
        check_vma=False,
    )
```

time: 219 us -> 170 us (0.78)
  blocking collectives: 107 us -> 52.1 us
  starting transfers between devices: 41.7 us -> 57.3 us
  Pallas kernels: 32.7 us -> 27.8 us
  waiting for transfers between devices: 25.7 us -> 23.2 us
    all_to_all x4 -> x3, blocking collectives: 80 us -> 52.1 us  [exchange(): return lax.all_to_all(array, axis, 0, 0, tiled=True)]
    all_gather x1 -> x0, blocking collectives: 27.2 us -> none  [body(): gather0 = lax.all_gather(scaled, 'z')]
    all_to_all x2 -> x4, starting transfers between devices: 9.28 us -> 36.1 us  [exchange(): return lax.all_to_all(array, axis, 0, 0, tiled=True)]
    ppermute x6, starting transfers between devices: 32.5 us -> 21.2 us  [swap(): return lax.ppermute(array, axis, [(0, 1), (1, 0)])]
    pallas_call x1, Pallas kernels: 18.4 us -> 7.27 us  [body(): call(whiten, (jax.ShapeDtypeStruct((width, rank), F32), jax.ShapeDtypeStr...]
    ppermute x6, waiting for transfers between devices: 18.4 us -> 8.37 us  [swap(): return lax.ppermute(array, axis, [(0, 1), (1, 0)])]
    all_to_all x2 -> x4, waiting for transfers between devices: 7.32 us -> 14.8 us  [exchange(): return lax.all_to_all(array, axis, 0, 0, tiled=True)]
    pallas_call x1 -> x3, Pallas kernels: 6.83 us -> 12.3 us  [the longest x1 7.68 us: body(): call(transposed_kernel, (part,) * 4, (SMEM, SMEM, HBM, HBM), (HBM,) * 4,...]
  transfers between devices with their start and end apart: 8 -> 10, of which waited for: 5 -> 7; matrix products, arithmetic and copies ran while one was open for 2% -> 3% of each run, Pallas kernels for 3% -> 10%
where the time goes in v2:
time: 170 us; the launch traced here: 168 us
  starting transfers between devices  57.3 us (34%)
  blocking collectives  52.1 us (31%)
  Pallas kernels  27.8 us (16%)
  waiting for transfers between devices  23.2 us (14%)
  other arithmetic  4.36 us (3%)
  local copies, waits for them, and re-layouts  2.86 us (2%)
    all_to_all x3, blocking collectives, exchange(): return lax.all_to_all(array, axis, 0, 0, tiled=True)  52.1 us
    all_to_all x4, starting transfers between devices, exchange(): return lax.all_to_all(array, axis, 0, 0, tiled=True)  36.1 us
    ppermute x6, starting transfers between devices, swap(): return lax.ppermute(array, axis, [(0, 1), (1, 0)])  21.2 us
    all_to_all x4, waiting for transfers between devices, exchange(): return lax.all_to_all(array, axis, 0, 0, tiled=True)  14.8 us
    ppermute x6, waiting for transfers between devices, swap(): return lax.ppermute(array, axis, [(0, 1), (1, 0)])  8.37 us
    pallas_call x1, Pallas kernels, body(): call(transposed_kernel, (part,) * 4, (SMEM, SMEM, HBM, HBM), (HBM,) * 4,...  7.68 us
    pallas_call x1, Pallas kernels, body(): call(whiten, (jax.ShapeDtypeStruct((width, rank), F32), jax.ShapeDtypeStr...  7.27 us
    pallas_call x1, Pallas kernels, body(): call(forward_kernel, jax.ShapeDtypeStruct((rows, width, rank), BF16), (SM...  6.28 us
  transfers between devices with their start and end apart: 10, of which 7 were waited for; matrix products, arithmetic and copies ran while one was open for 3% of the time, Pallas kernels for 10%

profile of v2, /device:TPU:1, one launch (start us, length us, event | category | flops | bytes accessed | tf_op | source)
XLA Modules:
  0.0 168.4 jit_solution(5783405745307300271)
XLA Ops:
  0.6 1.8 %scale.1 = (bf16[8,128,128]{2,1,0:T(8,128)(2,1)}, bf16[16,128,128]{2,1,0:T(8,128)(2,1)}) custom-call(bf16[128,128]{1,0:T(8,128)(2,1)} %bitcast.7, f32[1,128]{1,0:T(1,128)} %scale_ref.3), custom_call_target="tpu_custom_call" | custom-call | tf_op jit(solution)/shard_map/scale/pallas_call | solution.py:267
  2.4 5.9 %all-to-all-start = ((bf16[8,128,128]{2,1,0:T(8,128)(2,1)}), bf16[8,128,128]{2,1,0:T(8,128)(2,1)S(1)}, u32[]{:S(2)}, u32[]{:S(2)}) async-start(bf16[8,128,128]{2,1,0:T(8,128)(2,1)} %get-tuple-element.16), calls=%async_computation | async-start | bytes 524288 | tf_op jit(solution)/shard_map/all_to_all | solution.py:22
  9.6 2.8 %places.1.pos_ref = s32[152]{0:T(256)} custom-call(s32[256]{0:T(256)} %order_ref.1, s32[8,19]{1,0:T(8,128)} %bitcast.9, s32[8,1]{1,0:T(8,128)} %copy.11.count_ref), custom_call_target="tpu_custom_call" | custom-call | tf_op jit(solution)/shard_map/places/pallas_call | solution.py:283
  12.4 2.0 %all-to-all-done.own_hbm = bf16[8,128,128]{2,1,0:T(8,128)(2,1)S(1)} async-done(((bf16[8,128,128]{2,1,0:T(8,128)(2,1)}), bf16[8,128,128]{2,1,0:T(8,128)(2,1)S(1)}, u32[]{:S(2)}, u32[]{:S(2)}) %all-to-all-start) | async-done | bytes 262176 | tf_op jit(solution)/shard_map/all_to_all | solution.py:22
  14.4 15.1 %all-to-all-start.2 = ((bf16[16,128,128]{2,1,0:T(8,128)(2,1)}), bf16[16,128,128]{2,1,0:T(8,128)(2,1)S(1)}, u32[]{:S(2)}, u32[]{:S(2)}) async-start(bf16[16,128,128]{2,1,0:T(8,128)(2,1)} %get-tuple-element.22), calls=%async_computation.2 | async-start | bytes 1048576 | tf_op jit(solution)/shard_map/all_to_all | solution.py:22
  29.5 7.7 %transposed_products.1 = (f32[16,128,128]{2,1,0:T(8,128)}, f32[16,128,128]{2,1,0:T(8,128)}, f32[16,128,128]{2,1,0:T(8,128)}, f32[16,128,128]{2,1,0:T(8,128)}) custom-call(s32[152]{0:T(256)} %places.1.pos_ref, s32[8,1]{1,0:T(8,128)} %copy.11.count_ref, bf16[8,128,128]{2,1,0:T(8,128)(2,1)} %copy-done, bf16[8,1,19,128,128]{4,3,2,1,0:T(8,128)(2,1)} %rest_4_.1), custom_call_target="tpu_custom_call" | custom-call | tf_op jit(solution)/shard_map/transposed_products/pallas_call | solution.py:293
  37.2 4.5 %collective-permute-start.1 = (f32[16,128,128]{2,1,0:T(8,128)}, f32[16,128,128]{2,1,0:T(8,128)S(1)}, u32[]{:S(2)}, u32[]{:S(2)}) collective-permute-start(f32[16,128,128]{2,1,0:T(8,128)} %get-tuple-element.20), channel_id=1, source_target_pairs={{0,8},{8,0},{1,9},{9,1},{2,10},{10,2},{3,11},{11,3},{4,12},{12,4},... | collective-permute-start | bytes 3145736 | tf_op jit(solution)/shard_map/ppermute | solution.py:30
  41.7 1.9 %collective-permute-start = (f32[16,128,128]{2,1,0:T(8,128)}, f32[16,128,128]{2,1,0:T(8,128)S(1)}, u32[]{:S(2)}, u32[]{:S(2)}) collective-permute-start(f32[16,128,128]{2,1,0:T(8,128)} %get-tuple-element.18), channel_id=1, source_target_pairs={{0,8},{8,0},{1,9},{9,1},{2,10},{10,2},{3,11},{11,3},{4,12},{12,4},... | collective-permute-start | bytes 3145736 | tf_op jit(solution)/shard_map/ppermute | solution.py:30
  45.5 4.2 %collective-permute-start.2 = (bf16[16,128,128]{2,1,0:T(8,128)(2,1)S(1)}, bf16[16,128,128]{2,1,0:T(8,128)(2,1)S(1)}, u32[]{:S(2)}, u32[]{:S(2)}) collective-permute-start(bf16[16,128,128]{2,1,0:T(8,128)(2,1)S(1)} %add_convert_fusion.1), channel_id=1, source_target_pairs={{0,256},{256,0},{1,257},{257,1},{2,258},{258,2},{3,259},{259,3},{4... | collective-permute-start | bytes 1572872 | tf_op jit(solution)/shard_map/ppermute | solution.py:30
  51.6 4.5 %collective-permute-start.3 = (bf16[16,128,128]{2,1,0:T(8,128)(2,1)S(1)}, bf16[16,128,128]{2,1,0:T(8,128)(2,1)S(1)}, u32[]{:S(2)}, u32[]{:S(2)}) collective-permute-start(bf16[16,128,128]{2,1,0:T(8,128)(2,1)S(1)} %all-to-all-done.2.rest_0_), channel_id=1, source_target_pairs={{0,256},{256,0},{1,257},{257,1},{2,258},{258,2},{3,259},{259,3},{4... | collective-permute-start | bytes 1572872 | tf_op jit(solution)/shard_map/ppermute | solution.py:30
  56.1 6.0 %collective-permute-done.2 = bf16[16,128,128]{2,1,0:T(8,128)(2,1)S(1)} collective-permute-done((bf16[16,128,128]{2,1,0:T(8,128)(2,1)S(1)}, bf16[16,128,128]{2,1,0:T(8,128)(2,1)S(1)}, u32[]{:S(2)}, u32[]{:S(2)}) %collective-permute-start.2) | collective-permute-done | bytes 524320 | tf_op jit(solution)/shard_map/ppermute | solution.py:30
  63.0 11.7 %all-to-all-start.1 = ((bf16[16,128,128]{2,1,0:T(8,128)(2,1)}), bf16[16,128,128]{2,1,0:T(8,128)(2,1)S(1)}, u32[]{:S(2)}, u32[]{:S(2)}) async-start(bf16[16,128,128]{2,1,0:T(8,128)(2,1)} %add_convert_fusion), calls=%async_computation.1 | async-start | bytes 1048576 | tf_op jit(solution)/shard_map/all_to_all | solution.py:22
  74.7 4.2 %collective-permute-start.4 = (bf16[16,128,128]{2,1,0:T(8,128)(2,1)S(1)}, bf16[16,128,128]{2,1,0:T(8,128)(2,1)S(1)}, u32[]{:S(2)}, u32[]{:S(2)}) collective-permute-start(bf16[16,128,128]{2,1,0:T(8,128)(2,1)S(1)} %all-to-all-done.2.rest_0_), channel_id=1, source_target_pairs={{0,8},{8,0},{1,9},{9,1},{2,10},{10,2},{3,11},{11,3},{4,12},{12,4},... | collective-permute-start | bytes 1572872 | tf_op jit(solution)/shard_map/ppermute | solution.py:30
  78.9 1.9 %collective-permute-start.5 = (bf16[16,128,128]{2,1,0:T(8,128)(2,1)S(1)}, bf16[16,128,128]{2,1,0:T(8,128)(2,1)S(1)}, u32[]{:S(2)}, u32[]{:S(2)}) collective-permute-start(bf16[16,128,128]{2,1,0:T(8,128)(2,1)S(1)} %collective-permute-done.3.rest_1_), channel_id=1, source_target_pairs={{0,8},{8,0},{1,9},{9,1},{2,10},{10,2},{3,11},{11,3},{4,12},{12,4},... | collective-permute-start | bytes 1572872 | tf_op jit(solution)/shard_map/ppermute | solution.py:30
  80.9 1.9 %collective-permute-done.5.rest_3_ = bf16[16,128,128]{2,1,0:T(8,128)(2,1)S(1)} collective-permute-done((bf16[16,128,128]{2,1,0:T(8,128)(2,1)S(1)}, bf16[16,128,128]{2,1,0:T(8,128)(2,1)S(1)}, u32[]{:S(2)}, u32[]{:S(2)}) %collective-permute-start.5) | collective-permute-done | bytes 524320 | tf_op jit(solution)/shard_map/ppermute | solution.py:30
  83.6 6.3 %forward_products.1 = bf16[8,128,128]{2,1,0:T(8,128)(2,1)} custom-call(s32[152]{0:T(256)} %places.1.pos_ref, s32[8,1]{1,0:T(8,128)} %copy.11.count_ref, bf16[16,128,128]{2,1,0:T(8,128)(2,1)} %copy-done.2, bf16[16,128,128]{2,1,0:T(8,128)(2,1)} %copy-done.3, bf16[16,128,128]{2,1,0:T(8,128)(2,1)} %copy-done.4, bf16[16,128,128]{2,1,0:T(8,128)(2,1)} %copy-done.5, ...), custom_call_target="tpu_custom_call" | custom-call | flops 12650000384 | tf_op jit(solution)/shard_map/forward_products/pallas_call | solution.py:318
  89.8 6.9 %all-to-all-done.1 = bf16[16,128,128]{2,1,0:T(8,128)(2,1)S(1)} async-done(((bf16[16,128,128]{2,1,0:T(8,128)(2,1)}), bf16[16,128,128]{2,1,0:T(8,128)(2,1)S(1)}, u32[]{:S(2)}, u32[]{:S(2)}) %all-to-all-start.1) | async-done | bytes 524320 | tf_op jit(solution)/shard_map/all_to_all | solution.py:22
  96.8 3.4 %all-to-all-start.3 = ((bf16[8,128,128]{2,1,0:T(8,128)(2,1)}), bf16[8,128,128]{2,1,0:T(8,128)(2,1)S(1)}, u32[]{:S(2)}, u32[]{:S(2)}) async-start(bf16[8,128,128]{2,1,0:T(8,128)(2,1)} %forward_products.1), calls=%async_computation.3 | async-start | bytes 524288 | tf_op jit(solution)/shard_map/all_to_all | solution.py:22
  100.9 5.4 %all-to-all-done.3.fore_ref = bf16[8,128,128]{2,1,0:T(8,128)(2,1)S(1)} async-done(((bf16[8,128,128]{2,1,0:T(8,128)(2,1)}), bf16[8,128,128]{2,1,0:T(8,128)(2,1)S(1)}, u32[]{:S(2)}, u32[]{:S(2)}) %all-to-all-start.3) | async-done | bytes 262176 | tf_op jit(solution)/shard_map/all_to_all | solution.py:22
  107.0 2.0 %image_and_grams.1 = (f32[128,128]{1,0:T(8,128)}, f32[256,128]{1,0:T(8,128)}) custom-call(f32[128,128]{1,0:T(8,128)} %convert_reduce_fusion.back_ref, bf16[8,128,128]{2,1,0:T(8,128)(2,1)} %copy-done.1, bf16[128,128]{1,0:T(8,128)(2,1)} %bitcast.8, f32[1,128]{1,0:T(1,128)} %scale_ref.3), custom_call_target="tpu_custom_call" | custom-call | tf_op jit(solution)/shard_map/image_and_grams/pallas_call | solution.py:336
  109.0 20.8 %all_to_all.35 = f32[32,8,128]{2,1,0:T(8,128)S(1)} all-to-all(f32[32,8,128]{2,1,0:T(8,128)} %bitcast.6), channel_id=1, replica_groups=mesh['yh'=2,'z'=16,'core'=2,'yl'=2,'x'=4] {'yh','core','yl','x'}, dimensions={0} | all-to-all | bytes 262144 | tf_op jit(solution)/shard_map/all_to_all | solution.py:22
  129.8 18.1 %all_to_all.36 = f32[16,8,128]{2,1,0:T(8,128)S(1)} all-to-all(f32[16,8,128]{2,1,0:T(8,128)S(1)} %broadcast_in_dim.6), channel_id=1, replica_groups=mesh['yh'=2,'z'=16,'core'=2,'yl'=2,'x'=4] {'z'}, dimensions={0} | all-to-all | bytes 131072 | tf_op jit(solution)/shard_map/all_to_all | solution.py:22
  148.0 13.2 %all_to_all.37 = f32[32,8,128]{2,1,0:T(8,128)} all-to-all(f32[32,8,128]{2,1,0:T(8,128)S(1)} %broadcast_in_dim.7), channel_id=1, replica_groups=mesh['yh'=2,'z'=16,'core'=2,'yl'=2,'x'=4] {'yh','core','yl','x'}, dimensions={0} | all-to-all | bytes 262144 | tf_op jit(solution)/shard_map/all_to_all | solution.py:22
  161.2 7.3 %whiten.1 = (f32[128,128]{1,0:T(8,128)}, f32[128,128]{1,0:T(8,128)}) custom-call(f32[256,128]{1,0:T(8,128)} %bitcast.5, f32[128,128]{1,0:T(8,128)} %get-tuple-element.27.refs_1_), custom_call_target="tpu_custom_call" | custom-call | tf_op jit(solution)/shard_map/whiten/pallas_call | solution.py:353
  (26 shorter events, 8.3 us)
Async XLA Ops:
  2.4 12.0 %all-to-all-start = ((bf16[8,128,128]{2,1,0:T(8,128)(2,1)}), bf16[8,128,128]{2,1,0:T(8,128)(2,1)S(1)}, u32[]{:S(2)}, u32[]{:S(2)}) async-start(bf16[8,128,128]{2,1,0:T(8,128)(2,1)} %get-tuple-element.16), calls=%async_computation | async-start | bytes 524288 | tf_op jit(solution)/shard_map/all_to_all | solution.py:22
  14.4 15.1 %copy-start = (bf16[8,128,128]{2,1,0:T(8,128)(2,1)}, bf16[8,128,128]{2,1,0:T(8,128)(2,1)S(1)}, u32[]{:S(2)}) copy-start(bf16[8,128,128]{2,1,0:T(8,128)(2,1)S(1)} %all-to-all-done.own_hbm) | copy-start | bytes 786436
  14.4 37.1 %all-to-all-start.2 = ((bf16[16,128,128]{2,1,0:T(8,128)(2,1)}), bf16[16,128,128]{2,1,0:T(8,128)(2,1)S(1)}, u32[]{:S(2)}, u32[]{:S(2)}) async-start(bf16[16,128,128]{2,1,0:T(8,128)(2,1)} %get-tuple-element.22), calls=%async_computation.2 | async-start | bytes 1048576 | tf_op jit(solution)/shard_map/all_to_all | solution.py:22
  37.2 7.0 %collective-permute-start.1 = (f32[16,128,128]{2,1,0:T(8,128)}, f32[16,128,128]{2,1,0:T(8,128)S(1)}, u32[]{:S(2)}, u32[]{:S(2)}) collective-permute-start(f32[16,128,128]{2,1,0:T(8,128)} %get-tuple-element.20), channel_id=1, source_target_pairs={{0,8},{8,0},{1,9},{9,1},{2,10},{10,2},{3,11},{11,3},{4,12},{12,4},... | collective-permute-start | bytes 3145736 | tf_op jit(solution)/shard_map/ppermute | solution.py:30
  41.7 8.0 %collective-permute-start = (f32[16,128,128]{2,1,0:T(8,128)}, f32[16,128,128]{2,1,0:T(8,128)S(1)}, u32[]{:S(2)}, u32[]{:S(2)}) collective-permute-start(f32[16,128,128]{2,1,0:T(8,128)} %get-tuple-element.18), channel_id=1, source_target_pairs={{0,8},{8,0},{1,9},{9,1},{2,10},{10,2},{3,11},{11,3},{4,12},{12,4},... | collective-permute-start | bytes 3145736 | tf_op jit(solution)/shard_map/ppermute | solution.py:30
  45.5 16.5 %collective-permute-start.2 = (bf16[16,128,128]{2,1,0:T(8,128)(2,1)S(1)}, bf16[16,128,128]{2,1,0:T(8,128)(2,1)S(1)}, u32[]{:S(2)}, u32[]{:S(2)}) collective-permute-start(bf16[16,128,128]{2,1,0:T(8,128)(2,1)S(1)} %add_convert_fusion.1), channel_id=1, source_target_pairs={{0,256},{256,0},{1,257},{257,1},{2,258},{258,2},{3,259},{259,3},{4... | collective-permute-start | bytes 1572872 | tf_op jit(solution)/shard_map/ppermute | solution.py:30
  51.6 31.2 %copy-start.2 = (bf16[16,128,128]{2,1,0:T(8,128)(2,1)}, bf16[16,128,128]{2,1,0:T(8,128)(2,1)S(1)}, u32[]{:S(2)}) copy-start(bf16[16,128,128]{2,1,0:T(8,128)(2,1)S(1)} %all-to-all-done.2.rest_0_) | copy-start | bytes 1572868
  51.6 27.4 %collective-permute-start.3 = (bf16[16,128,128]{2,1,0:T(8,128)(2,1)S(1)}, bf16[16,128,128]{2,1,0:T(8,128)(2,1)S(1)}, u32[]{:S(2)}, u32[]{:S(2)}) collective-permute-start(bf16[16,128,128]{2,1,0:T(8,128)(2,1)S(1)} %all-to-all-done.2.rest_0_), channel_id=1, source_target_pairs={{0,256},{256,0},{1,257},{257,1},{2,258},{258,2},{3,259},{259,3},{4... | collective-permute-start | bytes 1572872 | tf_op jit(solution)/shard_map/ppermute | solution.py:30
  63.0 33.8 %all-to-all-start.1 = ((bf16[16,128,128]{2,1,0:T(8,128)(2,1)}), bf16[16,128,128]{2,1,0:T(8,128)(2,1)S(1)}, u32[]{:S(2)}, u32[]{:S(2)}) async-start(bf16[16,128,128]{2,1,0:T(8,128)(2,1)} %add_convert_fusion), calls=%async_computation.1 | async-start | bytes 1048576 | tf_op jit(solution)/shard_map/all_to_all | solution.py:22
  74.7 6.2 %collective-permute-start.4 = (bf16[16,128,128]{2,1,0:T(8,128)(2,1)S(1)}, bf16[16,128,128]{2,1,0:T(8,128)(2,1)S(1)}, u32[]{:S(2)}, u32[]{:S(2)}) collective-permute-start(bf16[16,128,128]{2,1,0:T(8,128)(2,1)S(1)} %all-to-all-done.2.rest_0_), channel_id=1, source_target_pairs={{0,8},{8,0},{1,9},{9,1},{2,10},{10,2},{3,11},{11,3},{4,12},{12,4},... | collective-permute-start | bytes 1572872 | tf_op jit(solution)/shard_map/ppermute | solution.py:30
  78.9 3.8 %copy-start.3 = (bf16[16,128,128]{2,1,0:T(8,128)(2,1)}, bf16[16,128,128]{2,1,0:T(8,128)(2,1)S(1)}, u32[]{:S(2)}) copy-start(bf16[16,128,128]{2,1,0:T(8,128)(2,1)S(1)} %collective-permute-done.3.rest_1_) | copy-start | bytes 1572868
  78.9 3.8 %collective-permute-start.5 = (bf16[16,128,128]{2,1,0:T(8,128)(2,1)S(1)}, bf16[16,128,128]{2,1,0:T(8,128)(2,1)S(1)}, u32[]{:S(2)}, u32[]{:S(2)}) collective-permute-start(bf16[16,128,128]{2,1,0:T(8,128)(2,1)S(1)} %collective-permute-done.3.rest_1_), channel_id=1, source_target_pairs={{0,8},{8,0},{1,9},{9,1},{2,10},{10,2},{3,11},{11,3},{4,12},{12,4},... | collective-permute-start | bytes 1572872 | tf_op jit(solution)/shard_map/ppermute | solution.py:30
  80.9 1.9 %copy-start.4 = (bf16[16,128,128]{2,1,0:T(8,128)(2,1)}, bf16[16,128,128]{2,1,0:T(8,128)(2,1)S(1)}, u32[]{:S(2)}) copy-start(bf16[16,128,128]{2,1,0:T(8,128)(2,1)S(1)} %collective-permute-done.4.rest_2_) | copy-start | bytes 1572868
  82.8 0.8 copy-start.5
  96.8 9.5 %all-to-all-start.3 = ((bf16[8,128,128]{2,1,0:T(8,128)(2,1)}), bf16[8,128,128]{2,1,0:T(8,128)(2,1)S(1)}, u32[]{:S(2)}, u32[]{:S(2)}) async-start(bf16[8,128,128]{2,1,0:T(8,128)(2,1)} %forward_products.1), calls=%async_computation.3 | async-start | bytes 524288 | tf_op jit(solution)/shard_map/all_to_all | solution.py:22
  106.3 0.7 copy-start.1

commit v3 on v2

--- a/solution.py
+++ b/solution.py
@@ -13,7 +13,8 @@
 PLANE = ("yh", "core", "yl", "x")
 GROUP = 19
 NO_COST = pl.CostEstimate(flops=0, bytes_accessed=0, transcendentals=0)
-VMEM_BYTES = 57 * 1024 * 1024
+VMEM_BYTES = 16 * 1024 * 1024
+TILE_VMEM_BYTES = 50 * 1024 * 1024
 F32 = jnp.float32
 BF16 = jnp.bfloat16
 
@@ -242,7 +243,7 @@
     return pl.BlockSpec(memory_space=space)
 
 
-def call(kernel, out_shape, in_spaces, out_spaces, scratch, name, cost=NO_COST):
+def call(kernel, out_shape, in_spaces, out_spaces, scratch, name, cost=NO_COST, vmem=VMEM_BYTES):
     many = isinstance(out_spaces, tuple)
     return pl.pallas_call(
         kernel,
@@ -250,7 +251,7 @@
         in_specs=[spec(s) for s in in_spaces],
         out_specs=tuple(spec(s) for s in out_spaces) if many else spec(out_spaces),
         scratch_shapes=scratch,
-        compiler_params=pltpu.CompilerParams(vmem_limit_bytes=VMEM_BYTES),
+        compiler_params=pltpu.CompilerParams(vmem_limit_bytes=vmem),
         cost_estimate=cost,
         name=name,
     )
@@ -304,6 +305,7 @@
             part_sems,
         ],
         "transposed_products",
+        vmem=TILE_VMEM_BYTES,
     )(places, tile_counts, own_rows, graph_tiles)
     far_got = swap(far_send, "core")
     near_got = swap(near_send, "core")
@@ -329,6 +331,7 @@
         ],
         "forward_products",
         pl.CostEstimate(flops=12650000000, bytes_accessed=0, transcendentals=0),
+        TILE_VMEM_BYTES,
     )(places, tile_counts, gather, gather1, gather2, gather3, graph_tiles)
     fore = exchange(after(forward, back), COL)
     back = back.astype(F32).sum(axis=0)

time: 170 us -> 163 us (0.959)
  Pallas kernels: 27.8 us -> 21.7 us
  other arithmetic: 4.36 us -> 1.31 us
  waiting for transfers between devices: 23.2 us -> 25.9 us
    all_to_all x4, waiting for transfers between devices: 14.8 us -> 21.2 us  [exchange(): return lax.all_to_all(array, axis, 0, 0, tiled=True)]
    ppermute x6, waiting for transfers between devices: 8.37 us -> 4.74 us  [swap(): return lax.ppermute(array, axis, [(0, 1), (1, 0)])]
    pallas_call x1, Pallas kernels: 7.68 us -> 5.62 us  [body(): call(transposed_kernel, (part,) * 4, (SMEM, SMEM, HBM, HBM), (HBM,) * 4,...]
  transfers between devices with their start and end apart: 10 -> 10, of which waited for: 7 -> 7; matrix products, arithmetic and copies ran while one was open for 3% -> 1% of each run, Pallas kernels for 10% -> 9%
where the time goes in v3:
time: 163 us; the launch traced here: 162 us
  starting transfers between devices  57.6 us (35%)
  blocking collectives  51.4 us (32%)
  waiting for transfers between devices  25.9 us (16%)
  Pallas kernels  21.7 us (13%)
  local copies, waits for them, and re-layouts  3.54 us (2%)
    all_to_all x3, blocking collectives, exchange(): return lax.all_to_all(array, axis, 0, 0, tiled=True)  51.4 us
    all_to_all x4, starting transfers between devices, exchange(): return lax.all_to_all(array, axis, 0, 0, tiled=True)  36.6 us
    all_to_all x4, waiting for transfers between devices, exchange(): return lax.all_to_all(array, axis, 0, 0, tiled=True)  21.2 us
    ppermute x6, starting transfers between devices, swap(): return lax.ppermute(array, axis, [(0, 1), (1, 0)])  21 us
    pallas_call x1, Pallas kernels, body(): call(whiten, (jax.ShapeDtypeStruct((width, rank), F32), jax.ShapeDtypeStr...  6.36 us
    pallas_call x1, Pallas kernels, body(): call(forward_kernel, jax.ShapeDtypeStruct((rows, width, rank), BF16), (SM...  5.66 us
    pallas_call x1, Pallas kernels, body(): call(transposed_kernel, (part,) * 4, (SMEM, SMEM, HBM, HBM), (HBM,) * 4,...  5.62 us
    ppermute x6, waiting for transfers between devices, swap(): return lax.ppermute(array, axis, [(0, 1), (1, 0)])  4.74 us
  transfers between devices with their start and end apart: 10, of which 7 were waited for; matrix products, arithmetic and copies ran while one was open for 1% of the time, Pallas kernels for 9%

profile of v3, /device:TPU:1, one launch (start us, length us, event | category | flops | bytes accessed | tf_op | source)
XLA Modules:
  0.0 162.3 jit_solution(13622907847186729052)
XLA Ops:
  2.0 1.0 scale.1
  3.1 5.9 %all-to-all-start = ((bf16[8,128,128]{2,1,0:T(8,128)(2,1)}), bf16[8,128,128]{2,1,0:T(8,128)(2,1)S(1)}, u32[]{:S(2)}, u32[]{:S(2)}) async-start(bf16[8,128,128]{2,1,0:T(8,128)(2,1)} %get-tuple-element.16), calls=%async_computation | async-start | bytes 524288 | tf_op jit(solution)/shard_map/all_to_all | solution.py:23
  11.0 2.7 %places.1.pos_ref = s32[152]{0:T(256)S(1)} custom-call(s32[256]{0:T(256)S(1)} %copy-done.5, s32[8,19]{1,0:T(8,128)S(1)} %bitcast.9, s32[8,1]{1,0:T(8,128)S(1)} %copy.11.count_ref), custom_call_target="tpu_custom_call" | custom-call | tf_op jit(solution)/shard_map/places/pallas_call | solution.py:284
  13.8 1.3 all-to-all-done.own_hbm
  15.1 15.1 %all-to-all-start.2 = ((bf16[16,128,128]{2,1,0:T(8,128)(2,1)}), bf16[16,128,128]{2,1,0:T(8,128)(2,1)S(1)}, u32[]{:S(2)}, u32[]{:S(2)}) async-start(bf16[16,128,128]{2,1,0:T(8,128)(2,1)} %get-tuple-element.22), calls=%async_computation.2 | async-start | bytes 1048576 | tf_op jit(solution)/shard_map/all_to_all | solution.py:23
  30.2 5.6 %transposed_products.1 = (f32[16,128,128]{2,1,0:T(8,128)S(1)}, f32[16,128,128]{2,1,0:T(8,128)S(1)}, f32[16,128,128]{2,1,0:T(8,128)S(1)}, f32[16,128,128]{2,1,0:T(8,128)}) custom-call(s32[152]{0:T(256)S(1)} %places.1.pos_ref, s32[8,1]{1,0:T(8,128)S(1)} %copy.11.count_ref, bf16[8,128,128]{2,1,0:T(8,128)(2,1)S(1)} %all-to-all-done.own_hbm, ...), custom_call_target="tpu_custom_call" | custom-call | tf_op jit(solution)/shard_map/transposed_products/pallas_call | solution.py:294
  35.8 4.1 %collective-permute-start.1 = (f32[16,128,128]{2,1,0:T(8,128)}, f32[16,128,128]{2,1,0:T(8,128)S(1)}, u32[]{:S(2)}, u32[]{:S(2)}) collective-permute-start(f32[16,128,128]{2,1,0:T(8,128)} %get-tuple-element.20), channel_id=1, source_target_pairs={{0,8},{8,0},{1,9},{9,1},{2,10},{10,2},{3,11},{11,3},{4,12},{12,4},... | collective-permute-start | bytes 3145736 | tf_op jit(solution)/shard_map/ppermute | solution.py:31
  39.9 1.9 %collective-permute-start = (f32[16,128,128]{2,1,0:T(8,128)S(1)}, f32[16,128,128]{2,1,0:T(8,128)S(1)}, u32[]{:S(2)}, u32[]{:S(2)}) collective-permute-start(f32[16,128,128]{2,1,0:T(8,128)S(1)} %get-tuple-element.18), channel_id=1, source_target_pairs={{0,8},{8,0},{1,9},{9,1},{2,10},{10,2},{3,11},{11,3},{4,12},{12,4},... | collective-permute-start | bytes 3145736 | tf_op jit(solution)/shard_map/ppermute | solution.py:31
  42.5 4.5 %collective-permute-start.2 = (bf16[16,128,128]{2,1,0:T(8,128)(2,1)S(1)}, bf16[16,128,128]{2,1,0:T(8,128)(2,1)S(1)}, u32[]{:S(2)}, u32[]{:S(2)}) collective-permute-start(bf16[16,128,128]{2,1,0:T(8,128)(2,1)S(1)} %add_convert_fusion.1), channel_id=1, source_target_pairs={{0,256},{256,0},{1,257},{257,1},{2,258},{258,2},{3,259},{259,3},{4... | collective-permute-start | bytes 1572872 | tf_op jit(solution)/shard_map/ppermute | solution.py:31
  47.2 5.0 %all-to-all-done.2.rest_0_ = bf16[16,128,128]{2,1,0:T(8,128)(2,1)S(1)} async-done(((bf16[16,128,128]{2,1,0:T(8,128)(2,1)}), bf16[16,128,128]{2,1,0:T(8,128)(2,1)S(1)}, u32[]{:S(2)}, u32[]{:S(2)}) %all-to-all-start.2) | async-done | bytes 524320 | tf_op jit(solution)/shard_map/all_to_all | solution.py:23
  52.2 4.5 %collective-permute-start.3 = (bf16[16,128,128]{2,1,0:T(8,128)(2,1)S(1)}, bf16[16,128,128]{2,1,0:T(8,128)(2,1)S(1)}, u32[]{:S(2)}, u32[]{:S(2)}) collective-permute-start(bf16[16,128,128]{2,1,0:T(8,128)(2,1)S(1)} %all-to-all-done.2.rest_0_), channel_id=1, source_target_pairs={{0,256},{256,0},{1,257},{257,1},{2,258},{258,2},{3,259},{259,3},{4... | collective-permute-start | bytes 1572872 | tf_op jit(solution)/shard_map/ppermute | solution.py:31
  56.7 2.3 %collective-permute-done.2 = bf16[16,128,128]{2,1,0:T(8,128)(2,1)S(1)} collective-permute-done((bf16[16,128,128]{2,1,0:T(8,128)(2,1)S(1)}, bf16[16,128,128]{2,1,0:T(8,128)(2,1)S(1)}, u32[]{:S(2)}, u32[]{:S(2)}) %collective-permute-start.2) | collective-permute-done | bytes 524320 | tf_op jit(solution)/shard_map/ppermute | solution.py:31
  60.0 12.1 %all-to-all-start.1 = ((bf16[16,128,128]{2,1,0:T(8,128)(2,1)}), bf16[16,128,128]{2,1,0:T(8,128)(2,1)S(1)}, u32[]{:S(2)}, u32[]{:S(2)}) async-start(bf16[16,128,128]{2,1,0:T(8,128)(2,1)} %add_convert_fusion), calls=%async_computation.1 | async-start | bytes 1048576 | tf_op jit(solution)/shard_map/all_to_all | solution.py:23
  72.1 3.9 %collective-permute-start.4 = (bf16[16,128,128]{2,1,0:T(8,128)(2,1)S(1)}, bf16[16,128,128]{2,1,0:T(8,128)(2,1)S(1)}, u32[]{:S(2)}, u32[]{:S(2)}) collective-permute-start(bf16[16,128,128]{2,1,0:T(8,128)(2,1)S(1)} %all-to-all-done.2.rest_0_), channel_id=1, source_target_pairs={{0,8},{8,0},{1,9},{9,1},{2,10},{10,2},{3,11},{11,3},{4,12},{12,4},... | collective-permute-start | bytes 1572872 | tf_op jit(solution)/shard_map/ppermute | solution.py:31
  76.1 1.9 %collective-permute-start.5 = (bf16[16,128,128]{2,1,0:T(8,128)(2,1)S(1)}, bf16[16,128,128]{2,1,0:T(8,128)(2,1)S(1)}, u32[]{:S(2)}, u32[]{:S(2)}) collective-permute-start(bf16[16,128,128]{2,1,0:T(8,128)(2,1)S(1)} %collective-permute-done.3.rest_1_), channel_id=1, source_target_pairs={{0,8},{8,0},{1,9},{9,1},{2,10},{10,2},{3,11},{11,3},{4,12},{12,4},... | collective-permute-start | bytes 1572872 | tf_op jit(solution)/shard_map/ppermute | solution.py:31
  78.0 1.9 %collective-permute-done.5.rest_3_ = bf16[16,128,128]{2,1,0:T(8,128)(2,1)S(1)} collective-permute-done((bf16[16,128,128]{2,1,0:T(8,128)(2,1)S(1)}, bf16[16,128,128]{2,1,0:T(8,128)(2,1)S(1)}, u32[]{:S(2)}, u32[]{:S(2)}) %collective-permute-start.5) | collective-permute-done | bytes 524320 | tf_op jit(solution)/shard_map/ppermute | solution.py:31
  79.9 5.7 %forward_products.1 = bf16[8,128,128]{2,1,0:T(8,128)(2,1)} custom-call(s32[152]{0:T(256)S(1)} %places.1.pos_ref, s32[8,1]{1,0:T(8,128)S(1)} %copy.11.count_ref, bf16[16,128,128]{2,1,0:T(8,128)(2,1)S(1)} %all-to-all-done.2.rest_0_, bf16[16,128,128]{2,1,0:T(8,128)(2,1)S(1)} %collective-permute-done.3.rest_1_, ...), custom_call_target="tpu_custom_call" | custom-call | flops 12650000384 | tf_op jit(solution)/shard_map/forward_products/pallas_call | solution.py:320
  85.6 8.8 %all-to-all-done.1 = bf16[16,128,128]{2,1,0:T(8,128)(2,1)S(1)} async-done(((bf16[16,128,128]{2,1,0:T(8,128)(2,1)}), bf16[16,128,128]{2,1,0:T(8,128)(2,1)S(1)}, u32[]{:S(2)}, u32[]{:S(2)}) %all-to-all-start.1) | async-done | bytes 524320 | tf_op jit(solution)/shard_map/all_to_all | solution.py:23
  94.4 3.6 %all-to-all-start.3 = ((bf16[8,128,128]{2,1,0:T(8,128)(2,1)}), bf16[8,128,128]{2,1,0:T(8,128)(2,1)S(1)}, u32[]{:S(2)}, u32[]{:S(2)}) async-start(bf16[8,128,128]{2,1,0:T(8,128)(2,1)} %forward_products.1), calls=%async_computation.3 | async-start | bytes 524288 | tf_op jit(solution)/shard_map/all_to_all | solution.py:23
  98.0 6.1 %all-to-all-done.3.fore_ref = bf16[8,128,128]{2,1,0:T(8,128)(2,1)S(1)} async-done(((bf16[8,128,128]{2,1,0:T(8,128)(2,1)}), bf16[8,128,128]{2,1,0:T(8,128)(2,1)S(1)}, u32[]{:S(2)}, u32[]{:S(2)}) %all-to-all-start.3) | async-done | bytes 262176 | tf_op jit(solution)/shard_map/all_to_all | solution.py:23
  104.4 20.6 %all_to_all.35 = f32[32,8,128]{2,1,0:T(8,128)S(1)} all-to-all(f32[32,8,128]{2,1,0:T(8,128)S(1)} %bitcast.6), channel_id=1, replica_groups=mesh['yh'=2,'z'=16,'core'=2,'yl'=2,'x'=4] {'yh','core','yl','x'}, dimensions={0} | all-to-all | bytes 262144 | tf_op jit(solution)/shard_map/all_to_all | solution.py:23
  125.1 17.8 %all_to_all.36 = f32[16,8,128]{2,1,0:T(8,128)S(1)} all-to-all(f32[16,8,128]{2,1,0:T(8,128)S(1)} %broadcast_in_dim.6), channel_id=1, replica_groups=mesh['yh'=2,'z'=16,'core'=2,'yl'=2,'x'=4] {'z'}, dimensions={0} | all-to-all | bytes 131072 | tf_op jit(solution)/shard_map/all_to_all | solution.py:23
  142.9 13.0 %all_to_all.37 = f32[32,8,128]{2,1,0:T(8,128)S(1)} all-to-all(f32[32,8,128]{2,1,0:T(8,128)S(1)} %broadcast_in_dim.7), channel_id=1, replica_groups=mesh['yh'=2,'z'=16,'core'=2,'yl'=2,'x'=4] {'yh','core','yl','x'}, dimensions={0} | all-to-all | bytes 262144 | tf_op jit(solution)/shard_map/all_to_all | solution.py:23
  155.9 6.4 %whiten.1 = (f32[128,128]{1,0:T(8,128)}, f32[128,128]{1,0:T(8,128)}) custom-call(f32[256,128]{1,0:T(8,128)S(1)} %bitcast.5, f32[128,128]{1,0:T(8,128)S(1)} %get-tuple-element.27.refs_1_), custom_call_target="tpu_custom_call" | custom-call | tf_op jit(solution)/shard_map/whiten/pallas_call | solution.py:356
  (26 shorter events, 5.8 us)
Async XLA Ops:
  0.6 0.8 copy-start
  1.4 0.7 copy-start.3
  3.1 12.0 %all-to-all-start = ((bf16[8,128,128]{2,1,0:T(8,128)(2,1)}), bf16[8,128,128]{2,1,0:T(8,128)(2,1)S(1)}, u32[]{:S(2)}, u32[]{:S(2)}) async-start(bf16[8,128,128]{2,1,0:T(8,128)(2,1)} %get-tuple-element.16), calls=%async_computation | async-start | bytes 524288 | tf_op jit(solution)/shard_map/all_to_all | solution.py:23
  9.7 0.7 copy-start.2
  10.4 0.7 copy-start.5
  15.1 37.1 %all-to-all-start.2 = ((bf16[16,128,128]{2,1,0:T(8,128)(2,1)}), bf16[16,128,128]{2,1,0:T(8,128)(2,1)S(1)}, u32[]{:S(2)}, u32[]{:S(2)}) async-start(bf16[16,128,128]{2,1,0:T(8,128)(2,1)} %get-tuple-element.22), calls=%async_computation.2 | async-start | bytes 1048576 | tf_op jit(solution)/shard_map/all_to_all | solution.py:23
  35.8 6.6 %collective-permute-start.1 = (f32[16,128,128]{2,1,0:T(8,128)}, f32[16,128,128]{2,1,0:T(8,128)S(1)}, u32[]{:S(2)}, u32[]{:S(2)}) collective-permute-start(f32[16,128,128]{2,1,0:T(8,128)} %get-tuple-element.20), channel_id=1, source_target_pairs={{0,8},{8,0},{1,9},{9,1},{2,10},{10,2},{3,11},{11,3},{4,12},{12,4},... | collective-permute-start | bytes 3145736 | tf_op jit(solution)/shard_map/ppermute | solution.py:31
  39.9 7.1 %collective-permute-start = (f32[16,128,128]{2,1,0:T(8,128)S(1)}, f32[16,128,128]{2,1,0:T(8,128)S(1)}, u32[]{:S(2)}, u32[]{:S(2)}) collective-permute-start(f32[16,128,128]{2,1,0:T(8,128)S(1)} %get-tuple-element.18), channel_id=1, source_target_pairs={{0,8},{8,0},{1,9},{9,1},{2,10},{10,2},{3,11},{11,3},{4,12},{12,4},... | collective-permute-start | bytes 3145736 | tf_op jit(solution)/shard_map/ppermute | solution.py:31
  42.5 16.5 %collective-permute-start.2 = (bf16[16,128,128]{2,1,0:T(8,128)(2,1)S(1)}, bf16[16,128,128]{2,1,0:T(8,128)(2,1)S(1)}, u32[]{:S(2)}, u32[]{:S(2)}) collective-permute-start(bf16[16,128,128]{2,1,0:T(8,128)(2,1)S(1)} %add_convert_fusion.1), channel_id=1, source_target_pairs={{0,256},{256,0},{1,257},{257,1},{2,258},{258,2},{3,259},{259,3},{4... | collective-permute-start | bytes 1572872 | tf_op jit(solution)/shard_map/ppermute | solution.py:31
  52.2 23.9 %collective-permute-start.3 = (bf16[16,128,128]{2,1,0:T(8,128)(2,1)S(1)}, bf16[16,128,128]{2,1,0:T(8,128)(2,1)S(1)}, u32[]{:S(2)}, u32[]{:S(2)}) collective-permute-start(bf16[16,128,128]{2,1,0:T(8,128)(2,1)S(1)} %all-to-all-done.2.rest_0_), channel_id=1, source_target_pairs={{0,256},{256,0},{1,257},{257,1},{2,258},{258,2},{3,259},{259,3},{4... | collective-permute-start | bytes 1572872 | tf_op jit(solution)/shard_map/ppermute | solution.py:31
  60.0 34.3 %all-to-all-start.1 = ((bf16[16,128,128]{2,1,0:T(8,128)(2,1)}), bf16[16,128,128]{2,1,0:T(8,128)(2,1)S(1)}, u32[]{:S(2)}, u32[]{:S(2)}) async-start(bf16[16,128,128]{2,1,0:T(8,128)(2,1)} %add_convert_fusion), calls=%async_computation.1 | async-start | bytes 1048576 | tf_op jit(solution)/shard_map/all_to_all | solution.py:23
  72.1 31.9 %copy-start.1 = (bf16[1,128,128]{2,1,0:T(8,128)(2,1)S(1)}, bf16[1,128,128]{2,1,0:T(8,128)(2,1)}, u32[]{:S(2)}) copy-start(bf16[1,128,128]{2,1,0:T(8,128)(2,1)} %param.10) | copy-start | bytes 98308
  72.1 31.9 %copy-start.4 = (f32[1,128]{1,0:T(1,128)S(1)}, f32[1,128]{1,0:T(1,128)}, u32[]{:S(2)}) copy-start(f32[1,128]{1,0:T(1,128)} %scale_ref.3) | copy-start | bytes 1540
  72.1 5.9 %collective-permute-start.4 = (bf16[16,128,128]{2,1,0:T(8,128)(2,1)S(1)}, bf16[16,128,128]{2,1,0:T(8,128)(2,1)S(1)}, u32[]{:S(2)}, u32[]{:S(2)}) collective-permute-start(bf16[16,128,128]{2,1,0:T(8,128)(2,1)S(1)} %all-to-all-done.2.rest_0_), channel_id=1, source_target_pairs={{0,8},{8,0},{1,9},{9,1},{2,10},{10,2},{3,11},{11,3},{4,12},{12,4},... | collective-permute-start | bytes 1572872 | tf_op jit(solution)/shard_map/ppermute | solution.py:31
  76.1 3.8 %collective-permute-start.5 = (bf16[16,128,128]{2,1,0:T(8,128)(2,1)S(1)}, bf16[16,128,128]{2,1,0:T(8,128)(2,1)S(1)}, u32[]{:S(2)}, u32[]{:S(2)}) collective-permute-start(bf16[16,128,128]{2,1,0:T(8,128)(2,1)S(1)} %collective-permute-done.3.rest_1_), channel_id=1, source_target_pairs={{0,8},{8,0},{1,9},{9,1},{2,10},{10,2},{3,11},{11,3},{4,12},{12,4},... | collective-permute-start | bytes 1572872 | tf_op jit(solution)/shard_map/ppermute | solution.py:31
  94.4 9.7 %all-to-all-start.3 = ((bf16[8,128,128]{2,1,0:T(8,128)(2,1)}), bf16[8,128,128]{2,1,0:T(8,128)(2,1)S(1)}, u32[]{:S(2)}, u32[]{:S(2)}) async-start(bf16[8,128,128]{2,1,0:T(8,128)(2,1)} %forward_products.1), calls=%async_computation.3 | async-start | bytes 524288 | tf_op jit(solution)/shard_map/all_to_all | solution.py:23

commit v4 on v3

--- a/solution.py
+++ b/solution.py
@@ -1,3 +1,5 @@
+import functools
+
 import jax
 import jax.numpy as jnp
 from jax import lax
@@ -31,6 +33,11 @@
     return lax.ppermute(array, axis, [(0, 1), (1, 0)])
 
 
+def shift(array, axis, step):
+    count = lax.axis_size(axis)
+    return lax.ppermute(array, axis, [(i, (i + step) % count) for i in range(count)])
+
+
 def after(array, *others):
     return lax.optimization_barrier((array, *others))[0]
 
@@ -121,7 +128,7 @@
 
 
 def forward_kernel(pos_ref, count_ref, *rest):
-    parts, (tiles_hbm, out_ref, tiles, blocks, total, tile_sems, part_sems) = rest[:4], rest[4:]
+    parts, (tiles_hbm, *outs, tiles, blocks, total, tile_sems, part_sems) = rest[:4], rest[4:]
     rows, slots = tiles.shape[0], tiles.shape[1]
     part = parts[0].shape[0]
     copies = [
@@ -130,42 +137,48 @@
     ]
     for copy in copies:
         copy.start()
-    ahead = 3
-    for q in range(ahead):
-        tile_copy(tiles_hbm, tiles, tile_sems, q).start()
+    across = len(outs)
+    own_half, here = lax.axis_index("yl"), lax.axis_index("x")
+    for step in range(across):
+        for i in range(2):
+            q = (own_half ^ i) * across + ((here + step) & (across - 1))
+            tile_copy(tiles_hbm, tiles, tile_sems, q).start()
     blocks[4 * part] = jnp.zeros(blocks.shape[1:], blocks.dtype)
     for copy in copies:
         copy.wait()
 
-    def one_row(q, carry):
+    def one_row(i, carry, step, out_ref):
+        q = (own_half ^ i) * across + ((here + step) & (across - 1))
         tile_copy(tiles_hbm, tiles, tile_sems, q).wait()
-
-        @pl.when(q + ahead < rows)
-        def _():
-            tile_copy(tiles_hbm, tiles, tile_sems, q + ahead).start()
-
-        count = count_ref[q, 0]
         total[...] = jnp.zeros_like(total)
         for first in range(0, slots, GROUP):
             group = range(first, min(first + GROUP, slots))
 
-            @pl.when(count > first)
+            @pl.when(count_ref[q, 0] > first)
             def _(group=group):
                 left = jnp.concatenate([tiles[q, s] for s in group], axis=1)
                 right = jnp.concatenate([blocks[pos_ref[q * slots + s]] for s in group], axis=0)
                 total[...] += jnp.dot(left, right, preferred_element_type=F32)
 
-        out_ref[q] = total[...].astype(out_ref.dtype)
+        out_ref[i] = total[...].astype(out_ref.dtype)
         return carry
 
-    lax.fori_loop(0, rows, one_row, 0)
-
-
-def image_kernel(back_ref, fore_ref, sketch_ref, scale_ref, image_ref, sums_ref):
+    for step, out_ref in enumerate(outs):
+        lax.fori_loop(0, 2, functools.partial(one_row, step=step, out_ref=out_ref), 0)
+
+
+def fore_kernel(keep_ref, *refs):
+    got, outs = refs[:-2], refs[-2:]
+    for i, out_ref in enumerate(outs):
+        total = keep_ref[i]
+        for ref in got:
+            total = total + ref[i].astype(F32)
+        out_ref[...] = total
+
+
+def image_kernel(back_ref, fore_ref, got_ref, sketch_ref, scale_ref, image_ref, sums_ref):
     back = back_ref[...]
-    fore = fore_ref[0].astype(F32)
-    for i in range(1, fore_ref.shape[0]):
-        fore = fore + fore_ref[i].astype(F32)
+    fore = fore_ref[...] + got_ref[...]
     sketch = sketch_ref[...].astype(F32)
     scale = jnp.broadcast_to(scale_ref[...], sketch.shape).T
     image = sketch - scale * (fore + back.T)
@@ -316,12 +329,13 @@
     gather1 = after(swap(gather, "yh"), back)
     gather2 = swap(gather, "core")
     gather3 = swap(gather1, "core")
-    back = exchange(back, "z")
-    forward = call(
+    back = exchange(after(back, gather2), "z")
+    pair = (2, width, rank)
+    fore, *sends = call(
         forward_kernel,
-        jax.ShapeDtypeStruct((rows, width, rank), BF16),
+        (jax.ShapeDtypeStruct(pair, F32),) + (jax.ShapeDtypeStruct(pair, BF16),) * 3,
         (SMEM, SMEM) + (HBM,) * 5,
-        VMEM,
+        (VMEM,) * 4,
         [
             tile_scratch,
             pltpu.VMEM((4 * z_count + 1, width, rank), BF16),
@@ -333,17 +347,20 @@
         pl.CostEstimate(flops=12650000000, bytes_accessed=0, transcendentals=0),
         TILE_VMEM_BYTES,
     )(places, tile_counts, gather, gather1, gather2, gather3, graph_tiles)
-    fore = exchange(after(forward, back), COL)
+    got = [shift(send, "x", step) for step, send in enumerate(sends, 1)]
+    whole = jax.ShapeDtypeStruct((width, rank), F32)
+    fore, other = call(fore_kernel, (whole,) * 2, (VMEM,) * 4, (VMEM,) * 2, [], "fore_sum")(fore, *got)
+    got = swap(other, "yl")
     back = back.astype(F32).sum(axis=0)
 
     image, sums = call(
         image_kernel,
         (jax.ShapeDtypeStruct((width, rank), F32), jax.ShapeDtypeStruct((2 * rank, rank), F32)),
-        (VMEM,) * 4,
+        (VMEM,) * 5,
         (VMEM,) * 2,
         [],
         "image_and_grams",
-    )(back, fore, sketch[0], degree_scale)
+    )(back, fore, got, sketch[0], degree_scale)
 
     pieces = lax.axis_size(PLANE)
     sums = exchange(sums.reshape(pieces, 2 * rank // pieces, rank), PLANE).sum(axis=0)

time: 163 us -> 160 us (0.982)
  waiting for transfers between devices: 25.9 us -> 13.8 us
  starting transfers between devices: 57.6 us -> 67.5 us
  blocking collectives: 51.4 us -> 48.9 us
  other arithmetic: 1.31 us -> 3.57 us
    all_to_all x4 -> x3, waiting for transfers between devices: 21.2 us -> 6.1 us  [exchange(): return lax.all_to_all(array, axis, 0, 0, tiled=True)]
    ppermute x0 -> x3, starting transfers between devices: none -> 9.77 us  [shift(): lax.ppermute(array, axis, [(i, (i + step) % count) for i in range(count)])]
    ppermute x6 -> x7, starting transfers between devices: 21 us -> 30 us  [swap(): return lax.ppermute(array, axis, [(0, 1), (1, 0)])]
    all_to_all x4 -> x3, starting transfers between devices: 36.6 us -> 27.7 us  [exchange(): return lax.all_to_all(array, axis, 0, 0, tiled=True)]
    all_to_all x3, blocking collectives: 51.4 us -> 48.9 us  [exchange(): return lax.all_to_all(array, axis, 0, 0, tiled=True)]
    ppermute x6 -> x7, waiting for transfers between devices: 4.74 us -> 6.43 us  [swap(): return lax.ppermute(array, axis, [(0, 1), (1, 0)])]
    pallas_call x1 -> x2, Pallas kernels: 5.66 us -> 4.68 us  [the longest x1 4.64 us: body(): call(forward_kernel, (jax.ShapeDtypeStruct(pair, F32),) + (jax.ShapeDtype...]
  transfers between devices with their start and end apart: 10 -> 13, of which waited for: 7 -> 7; matrix products, arithmetic and copies ran while one was open for 1% -> 3% of each run, Pallas kernels for 9% -> 8%
where the time goes in v4:
time: 160 us; the launch traced here: 159 us
  starting transfers between devices  67.5 us (42%)
  blocking collectives  48.9 us (31%)
  Pallas kernels  21.1 us (13%)
  waiting for transfers between devices  13.8 us (9%)
  other arithmetic  3.57 us (2%)
  local copies, waits for them, and re-layouts  3.54 us (2%)
    all_to_all x3, blocking collectives, exchange(): return lax.all_to_all(array, axis, 0, 0, tiled=True)  48.9 us
    ppermute x7, starting transfers between devices, swap(): return lax.ppermute(array, axis, [(0, 1), (1, 0)])  30 us
    all_to_all x3, starting transfers between devices, exchange(): return lax.all_to_all(array, axis, 0, 0, tiled=True)  27.7 us
    ppermute x3, starting transfers between devices, shift(): lax.ppermute(array, axis, [(i, (i + step) % count) for i in range(count)])  9.77 us
    ppermute x7, waiting for transfers between devices, swap(): return lax.ppermute(array, axis, [(0, 1), (1, 0)])  6.43 us
    pallas_call x1, Pallas kernels, body(): call(whiten, (jax.ShapeDtypeStruct((width, rank), F32), jax.ShapeDtypeStr...  6.36 us
    all_to_all x3, waiting for transfers between devices, exchange(): return lax.all_to_all(array, axis, 0, 0, tiled=True)  6.1 us
    pallas_call x1, Pallas kernels, body(): call(transposed_kernel, (part,) * 4, (SMEM, SMEM, HBM, HBM), (HBM,) * 4,...  5.98 us
  transfers between devices with their start and end apart: 13, of which 7 were waited for; matrix products, arithmetic and copies ran while one was open for 3% of the time, Pallas kernels for 8%

profile of v4, /device:TPU:1, one launch (start us, length us, event | category | flops | bytes accessed | tf_op | source)
XLA Modules:
  0.0 159.3 jit_solution(9622813508344300923)
XLA Ops:
  3.0 5.9 %all-to-all-start = ((bf16[8,128,128]{2,1,0:T(8,128)(2,1)}), bf16[8,128,128]{2,1,0:T(8,128)(2,1)S(1)}, u32[]{:S(2)}, u32[]{:S(2)}) async-start(bf16[8,128,128]{2,1,0:T(8,128)(2,1)} %get-tuple-element.22), calls=%async_computation | async-start | bytes 524288 | tf_op jit(solution)/shard_map/all_to_all | solution.py:25
  11.0 2.7 %places.1.pos_ref = s32[152]{0:T(256)S(1)} custom-call(s32[256]{0:T(256)S(1)} %copy-done.5, s32[8,19]{1,0:T(8,128)S(1)} %bitcast.9, s32[8,1]{1,0:T(8,128)S(1)} %copy.11.count_ref), custom_call_target="tpu_custom_call" | custom-call | tf_op jit(solution)/shard_map/places/pallas_call | solution.py:297
  15.0 15.1 %all-to-all-start.1 = ((bf16[16,128,128]{2,1,0:T(8,128)(2,1)}), bf16[16,128,128]{2,1,0:T(8,128)(2,1)S(1)}, u32[]{:S(2)}, u32[]{:S(2)}) async-start(bf16[16,128,128]{2,1,0:T(8,128)(2,1)} %get-tuple-element.28), calls=%async_computation.1 | async-start | bytes 1048576 | tf_op jit(solution)/shard_map/all_to_all | solution.py:25
  30.1 6.0 %transposed_products.1 = (f32[16,128,128]{2,1,0:T(8,128)S(1)}, f32[16,128,128]{2,1,0:T(8,128)S(1)}, f32[16,128,128]{2,1,0:T(8,128)S(1)}, f32[16,128,128]{2,1,0:T(8,128)}) custom-call(s32[152]{0:T(256)S(1)} %places.1.pos_ref, s32[8,1]{1,0:T(8,128)S(1)} %copy.11.count_ref, bf16[8,128,128]{2,1,0:T(8,128)(2,1)S(1)} %all-to-all-done.own_hbm, ...), custom_call_target="tpu_custom_call" | custom-call | tf_op jit(solution)/shard_map/transposed_products/pallas_call | solution.py:307
  36.1 4.1 %collective-permute-start.1 = (f32[16,128,128]{2,1,0:T(8,128)}, f32[16,128,128]{2,1,0:T(8,128)S(1)}, u32[]{:S(2)}, u32[]{:S(2)}) collective-permute-start(f32[16,128,128]{2,1,0:T(8,128)} %get-tuple-element.26), channel_id=1, source_target_pairs={{0,8},{8,0},{1,9},{9,1},{2,10},{10,2},{3,11},{11,3},{4,12},{12,4},... | collective-permute-start | bytes 3145736 | tf_op jit(solution)/shard_map/ppermute | solution.py:33
  40.3 1.9 %collective-permute-start = (f32[16,128,128]{2,1,0:T(8,128)S(1)}, f32[16,128,128]{2,1,0:T(8,128)}, u32[]{:S(2)}, u32[]{:S(2)}) collective-permute-start(f32[16,128,128]{2,1,0:T(8,128)S(1)} %get-tuple-element.24), channel_id=1, source_target_pairs={{0,8},{8,0},{1,9},{9,1},{2,10},{10,2},{3,11},{11,3},{4,12},{12,4},... | collective-permute-start | bytes 3145736 | tf_op jit(solution)/shard_map/ppermute | solution.py:33
  42.9 4.5 %collective-permute-start.2 = (bf16[16,128,128]{2,1,0:T(8,128)(2,1)S(1)}, bf16[16,128,128]{2,1,0:T(8,128)(2,1)}, u32[]{:S(2)}, u32[]{:S(2)}) collective-permute-start(bf16[16,128,128]{2,1,0:T(8,128)(2,1)S(1)} %add_convert_fusion.1), channel_id=1, source_target_pairs={{0,256},{256,0},{1,257},{257,1},{2,258},{258,2},{3,259},{259,3},{4... | collective-permute-start | bytes 1572872 | tf_op jit(solution)/shard_map/ppermute | solution.py:33
  47.4 4.8 %all-to-all-done.1.rest_0_ = bf16[16,128,128]{2,1,0:T(8,128)(2,1)S(1)} async-done(((bf16[16,128,128]{2,1,0:T(8,128)(2,1)}), bf16[16,128,128]{2,1,0:T(8,128)(2,1)S(1)}, u32[]{:S(2)}, u32[]{:S(2)}) %all-to-all-start.1) | async-done | bytes 524320 | tf_op jit(solution)/shard_map/all_to_all | solution.py:25
  52.2 9.1 %collective-permute-start.3 = (bf16[16,128,128]{2,1,0:T(8,128)(2,1)S(1)}, bf16[16,128,128]{2,1,0:T(8,128)(2,1)S(1)}, u32[]{:S(2)}, u32[]{:S(2)}) collective-permute-start(bf16[16,128,128]{2,1,0:T(8,128)(2,1)S(1)} %all-to-all-done.1.rest_0_), channel_id=1, source_target_pairs={{0,8},{8,0},{1,9},{9,1},{2,10},{10,2},{3,11},{11,3},{4,12},{12,4},... | collective-permute-start | bytes 1572872 | tf_op jit(solution)/shard_map/ppermute | solution.py:33
  61.3 4.5 %collective-permute-start.4 = (bf16[16,128,128]{2,1,0:T(8,128)(2,1)S(1)}, bf16[16,128,128]{2,1,0:T(8,128)(2,1)S(1)}, u32[]{:S(2)}, u32[]{:S(2)}) collective-permute-start(bf16[16,128,128]{2,1,0:T(8,128)(2,1)S(1)} %all-to-all-done.1.rest_0_), channel_id=1, source_target_pairs={{0,256},{256,0},{1,257},{257,1},{2,258},{258,2},{3,259},{259,3},{4... | collective-permute-start | bytes 1572872 | tf_op jit(solution)/shard_map/ppermute | solution.py:33
  67.2 2.0 %add_convert_fusion = bf16[16,128,128]{2,1,0:T(8,128)(2,1)} fusion(f32[16,128,128]{2,1,0:T(8,128)S(1)} %add.9, bf16[16,128,128]{2,1,0:T(8,128)(2,1)} %collective-permute-done.2), kind=kLoop, calls=%fused_computation.1 | loop fusion | flops 786432 | bytes 2097152 | tf_op jit(solution)/shard_map/convert_element_type | solution.py:327
  69.2 6.8 %all-to-all-start.2 = ((bf16[16,128,128]{2,1,0:T(8,128)(2,1)}), bf16[16,128,128]{2,1,0:T(8,128)(2,1)S(1)}, u32[]{:S(2)}, u32[]{:S(2)}) async-start(bf16[16,128,128]{2,1,0:T(8,128)(2,1)} %add_convert_fusion), calls=%async_computation.2 | async-start | bytes 1048576 | tf_op jit(solution)/shard_map/all_to_all | solution.py:25
  76.0 2.2 %collective-permute-done.4.rest_1_ = bf16[16,128,128]{2,1,0:T(8,128)(2,1)S(1)} collective-permute-done((bf16[16,128,128]{2,1,0:T(8,128)(2,1)S(1)}, bf16[16,128,128]{2,1,0:T(8,128)(2,1)S(1)}, u32[]{:S(2)}, u32[]{:S(2)}) %collective-permute-start.4) | collective-permute-done | bytes 524320 | tf_op jit(solution)/shard_map/ppermute | solution.py:33
  78.3 2.7 %collective-permute-start.5 = (bf16[16,128,128]{2,1,0:T(8,128)(2,1)S(1)}, bf16[16,128,128]{2,1,0:T(8,128)(2,1)S(1)}, u32[]{:S(2)}, u32[]{:S(2)}) collective-permute-start(bf16[16,128,128]{2,1,0:T(8,128)(2,1)S(1)} %collective-permute-done.4.rest_1_), channel_id=1, source_target_pairs={{0,8},{8,0},{1,9},{9,1},{2,10},{10,2},{3,11},{11,3},{4,12},{12,4},... | collective-permute-start | bytes 1572872 | tf_op jit(solution)/shard_map/ppermute | solution.py:33
  82.5 4.6 %forward_products.1 = (f32[2,128,128]{2,1,0:T(8,128)S(1)}, bf16[2,128,128]{2,1,0:T(8,128)(2,1)S(1)}, bf16[2,128,128]{2,1,0:T(8,128)(2,1)S(1)}, bf16[2,128,128]{2,1,0:T(8,128)(2,1)S(1)}) custom-call(s32[152]{0:T(256)S(1)} %places.1.pos_ref, s32[8,1]{1,0:T(8,128)S(1)} %copy.11.count_ref, bf16[16,128,128]{2,1,0:T(8,128)(2,1)S(1)} %all-to-all-done.1.rest_0_, ...), custom_call_target="tpu_custom_call" | custom-call | flops 12650000384 | tf_op jit(solution)/shard_map/forward_products/pallas_call | solution.py:334
  87.1 1.9 %collective-permute-start.6 = (bf16[2,128,128]{2,1,0:T(8,128)(2,1)S(1)}, bf16[2,128,128]{2,1,0:T(8,128)(2,1)S(1)}, u32[]{:S(2)}, u32[]{:S(2)}) collective-permute-start(bf16[2,128,128]{2,1,0:T(8,128)(2,1)S(1)} %get-tuple-element.33), channel_id=1, source_target_pairs={{0,1},{1,2},{2,3},{3,0},{4,5},{5,6},{6,7},{7,4},{8,9},{9,10},{10,1... | collective-permute-start | bytes 196616 | tf_op jit(solution)/shard_map/ppermute | solution.py:38
  89.0 3.9 %collective-permute-start.7 = (bf16[2,128,128]{2,1,0:T(8,128)(2,1)S(1)}, bf16[2,128,128]{2,1,0:T(8,128)(2,1)S(1)}, u32[]{:S(2)}, u32[]{:S(2)}) collective-permute-start(bf16[2,128,128]{2,1,0:T(8,128)(2,1)S(1)} %get-tuple-element.34), channel_id=1, source_target_pairs={{0,2},{1,3},{2,0},{3,1},{4,6},{5,7},{6,4},{7,5},{8,10},{9,11},{10,... | collective-permute-start | bytes 196616 | tf_op jit(solution)/shard_map/ppermute | solution.py:38
  92.9 4.0 %collective-permute-start.8 = (bf16[2,128,128]{2,1,0:T(8,128)(2,1)S(1)}, bf16[2,128,128]{2,1,0:T(8,128)(2,1)S(1)}, u32[]{:S(2)}, u32[]{:S(2)}) collective-permute-start(bf16[2,128,128]{2,1,0:T(8,128)(2,1)S(1)} %get-tuple-element.35), channel_id=1, source_target_pairs={{0,3},{1,0},{2,1},{3,2},{4,7},{5,4},{6,5},{7,6},{8,11},{9,8},{10,9... | collective-permute-start | bytes 196616 | tf_op jit(solution)/shard_map/ppermute | solution.py:38
  98.3 3.1 %collective-permute-start.9 = (f32[128,128]{1,0:T(8,128)S(1)}, f32[128,128]{1,0:T(8,128)S(1)}, u32[]{:S(2)}, u32[]{:S(2)}) collective-permute-start(f32[128,128]{1,0:T(8,128)S(1)} %get-tuple-element.37), channel_id=1, source_target_pairs={{0,4},{4,0},{1,5},{5,1},{2,6},{6,2},{3,7},{7,3},{8,12},{12,8},{9,1... | collective-permute-start | bytes 196616 | tf_op jit(solution)/shard_map/ppermute | solution.py:33
  101.5 2.1 %collective-permute-done.9.got_ref = f32[128,128]{1,0:T(8,128)S(1)} collective-permute-done((f32[128,128]{1,0:T(8,128)S(1)}, f32[128,128]{1,0:T(8,128)S(1)}, u32[]{:S(2)}, u32[]{:S(2)}) %collective-permute-start.9) | collective-permute-done | bytes 65568 | tf_op jit(solution)/shard_map/ppermute | solution.py:33
  104.0 17.3 %all_to_all.30 = f32[32,8,128]{2,1,0:T(8,128)S(1)} all-to-all(f32[32,8,128]{2,1,0:T(8,128)S(1)} %bitcast.8), channel_id=1, replica_groups=mesh['yh'=2,'z'=16,'core'=2,'yl'=2,'x'=4] {'yh','core','yl','x'}, dimensions={0} | all-to-all | bytes 262144 | tf_op jit(solution)/shard_map/all_to_all | solution.py:25
  121.3 18.5 %all_to_all.31 = f32[16,8,128]{2,1,0:T(8,128)S(1)} all-to-all(f32[16,8,128]{2,1,0:T(8,128)S(1)} %broadcast_in_dim.6), channel_id=1, replica_groups=mesh['yh'=2,'z'=16,'core'=2,'yl'=2,'x'=4] {'z'}, dimensions={0} | all-to-all | bytes 131072 | tf_op jit(solution)/shard_map/all_to_all | solution.py:25
  139.9 13.0 %all_to_all.32 = f32[32,8,128]{2,1,0:T(8,128)S(1)} all-to-all(f32[32,8,128]{2,1,0:T(8,128)S(1)} %broadcast_in_dim.7), channel_id=1, replica_groups=mesh['yh'=2,'z'=16,'core'=2,'yl'=2,'x'=4] {'yh','core','yl','x'}, dimensions={0} | all-to-all | bytes 262144 | tf_op jit(solution)/shard_map/all_to_all | solution.py:25
  153.0 6.4 %whiten.1 = (f32[128,128]{1,0:T(8,128)}, f32[128,128]{1,0:T(8,128)}) custom-call(f32[256,128]{1,0:T(8,128)S(1)} %bitcast.5, f32[128,128]{1,0:T(8,128)S(1)} %get-tuple-element.39.refs_1_), custom_call_target="tpu_custom_call" | custom-call | tf_op jit(solution)/shard_map/whiten/pallas_call | solution.py:373
  (33 shorter events, 11.2 us)
Async XLA Ops:
  0.6 0.8 copy-start
  1.4 0.7 copy-start.3
  3.0 12.0 %all-to-all-start = ((bf16[8,128,128]{2,1,0:T(8,128)(2,1)}), bf16[8,128,128]{2,1,0:T(8,128)(2,1)S(1)}, u32[]{:S(2)}, u32[]{:S(2)}) async-start(bf16[8,128,128]{2,1,0:T(8,128)(2,1)} %get-tuple-element.22), calls=%async_computation | async-start | bytes 524288 | tf_op jit(solution)/shard_map/all_to_all | solution.py:25
  9.6 0.7 copy-start.2
  10.3 0.7 copy-start.5
  15.0 37.1 %all-to-all-start.1 = ((bf16[16,128,128]{2,1,0:T(8,128)(2,1)}), bf16[16,128,128]{2,1,0:T(8,128)(2,1)S(1)}, u32[]{:S(2)}, u32[]{:S(2)}) async-start(bf16[16,128,128]{2,1,0:T(8,128)(2,1)} %get-tuple-element.28), calls=%async_computation.1 | async-start | bytes 1048576 | tf_op jit(solution)/shard_map/all_to_all | solution.py:25
  36.1 6.6 %collective-permute-start.1 = (f32[16,128,128]{2,1,0:T(8,128)}, f32[16,128,128]{2,1,0:T(8,128)S(1)}, u32[]{:S(2)}, u32[]{:S(2)}) collective-permute-start(f32[16,128,128]{2,1,0:T(8,128)} %get-tuple-element.26), channel_id=1, source_target_pairs={{0,8},{8,0},{1,9},{9,1},{2,10},{10,2},{3,11},{11,3},{4,12},{12,4},... | collective-permute-start | bytes 3145736 | tf_op jit(solution)/shard_map/ppermute | solution.py:33
  40.3 7.1 %collective-permute-start = (f32[16,128,128]{2,1,0:T(8,128)S(1)}, f32[16,128,128]{2,1,0:T(8,128)}, u32[]{:S(2)}, u32[]{:S(2)}) collective-permute-start(f32[16,128,128]{2,1,0:T(8,128)S(1)} %get-tuple-element.24), channel_id=1, source_target_pairs={{0,8},{8,0},{1,9},{9,1},{2,10},{10,2},{3,11},{11,3},{4,12},{12,4},... | collective-permute-start | bytes 3145736 | tf_op jit(solution)/shard_map/ppermute | solution.py:33
  42.9 24.3 %collective-permute-start.2 = (bf16[16,128,128]{2,1,0:T(8,128)(2,1)S(1)}, bf16[16,128,128]{2,1,0:T(8,128)(2,1)}, u32[]{:S(2)}, u32[]{:S(2)}) collective-permute-start(bf16[16,128,128]{2,1,0:T(8,128)(2,1)S(1)} %add_convert_fusion.1), channel_id=1, source_target_pairs={{0,256},{256,0},{1,257},{257,1},{2,258},{258,2},{3,259},{259,3},{4... | collective-permute-start | bytes 1572872 | tf_op jit(solution)/shard_map/ppermute | solution.py:33
  52.2 17.0 %collective-permute-start.3 = (bf16[16,128,128]{2,1,0:T(8,128)(2,1)S(1)}, bf16[16,128,128]{2,1,0:T(8,128)(2,1)S(1)}, u32[]{:S(2)}, u32[]{:S(2)}) collective-permute-start(bf16[16,128,128]{2,1,0:T(8,128)(2,1)S(1)} %all-to-all-done.1.rest_0_), channel_id=1, source_target_pairs={{0,8},{8,0},{1,9},{9,1},{2,10},{10,2},{3,11},{11,3},{4,12},{12,4},... | collective-permute-start | bytes 1572872 | tf_op jit(solution)/shard_map/ppermute | solution.py:33
  61.3 16.9 %collective-permute-start.4 = (bf16[16,128,128]{2,1,0:T(8,128)(2,1)S(1)}, bf16[16,128,128]{2,1,0:T(8,128)(2,1)S(1)}, u32[]{:S(2)}, u32[]{:S(2)}) collective-permute-start(bf16[16,128,128]{2,1,0:T(8,128)(2,1)S(1)} %all-to-all-done.1.rest_0_), channel_id=1, source_target_pairs={{0,256},{256,0},{1,257},{257,1},{2,258},{258,2},{3,259},{259,3},{4... | collective-permute-start | bytes 1572872 | tf_op jit(solution)/shard_map/ppermute | solution.py:33
  69.2 32.2 %all-to-all-start.2 = ((bf16[16,128,128]{2,1,0:T(8,128)(2,1)}), bf16[16,128,128]{2,1,0:T(8,128)(2,1)S(1)}, u32[]{:S(2)}, u32[]{:S(2)}) async-start(bf16[16,128,128]{2,1,0:T(8,128)(2,1)} %add_convert_fusion), calls=%async_computation.2 | async-start | bytes 1048576 | tf_op jit(solution)/shard_map/all_to_all | solution.py:25
  76.0 27.6 %copy-start.1 = (bf16[1,128,128]{2,1,0:T(8,128)(2,1)S(1)}, bf16[1,128,128]{2,1,0:T(8,128)(2,1)}, u32[]{:S(2)}) copy-start(bf16[1,128,128]{2,1,0:T(8,128)(2,1)} %param.10) | copy-start | bytes 98308
  76.0 27.6 %copy-start.4 = (f32[1,128]{1,0:T(1,128)S(1)}, f32[1,128]{1,0:T(1,128)}, u32[]{:S(2)}) copy-start(f32[1,128]{1,0:T(1,128)} %scale_ref.3) | copy-start | bytes 1540
  78.3 4.2 %collective-permute-start.5 = (bf16[16,128,128]{2,1,0:T(8,128)(2,1)S(1)}, bf16[16,128,128]{2,1,0:T(8,128)(2,1)S(1)}, u32[]{:S(2)}, u32[]{:S(2)}) collective-permute-start(bf16[16,128,128]{2,1,0:T(8,128)(2,1)S(1)} %collective-permute-done.4.rest_1_), channel_id=1, source_target_pairs={{0,8},{8,0},{1,9},{9,1},{2,10},{10,2},{3,11},{11,3},{4,12},{12,4},... | collective-permute-start | bytes 1572872 | tf_op jit(solution)/shard_map/ppermute | solution.py:33
  87.1 9.8 %collective-permute-start.6 = (bf16[2,128,128]{2,1,0:T(8,128)(2,1)S(1)}, bf16[2,128,128]{2,1,0:T(8,128)(2,1)S(1)}, u32[]{:S(2)}, u32[]{:S(2)}) collective-permute-start(bf16[2,128,128]{2,1,0:T(8,128)(2,1)S(1)} %get-tuple-element.33), channel_id=1, source_target_pairs={{0,1},{1,2},{2,3},{3,0},{4,5},{5,6},{6,7},{7,4},{8,9},{9,10},{10,1... | collective-permute-start | bytes 196616 | tf_op jit(solution)/shard_map/ppermute | solution.py:38
  89.0 7.9 %collective-permute-start.7 = (bf16[2,128,128]{2,1,0:T(8,128)(2,1)S(1)}, bf16[2,128,128]{2,1,0:T(8,128)(2,1)S(1)}, u32[]{:S(2)}, u32[]{:S(2)}) collective-permute-start(bf16[2,128,128]{2,1,0:T(8,128)(2,1)S(1)} %get-tuple-element.34), channel_id=1, source_target_pairs={{0,2},{1,3},{2,0},{3,1},{4,6},{5,7},{6,4},{7,5},{8,10},{9,11},{10,... | collective-permute-start | bytes 196616 | tf_op jit(solution)/shard_map/ppermute | solution.py:38
  92.9 5.3 %collective-permute-start.8 = (bf16[2,128,128]{2,1,0:T(8,128)(2,1)S(1)}, bf16[2,128,128]{2,1,0:T(8,128)(2,1)S(1)}, u32[]{:S(2)}, u32[]{:S(2)}) collective-permute-start(bf16[2,128,128]{2,1,0:T(8,128)(2,1)S(1)} %get-tuple-element.35), channel_id=1, source_target_pairs={{0,3},{1,0},{2,1},{3,2},{4,7},{5,4},{6,5},{7,6},{8,11},{9,8},{10,9... | collective-permute-start | bytes 196616 | tf_op jit(solution)/shard_map/ppermute | solution.py:38
  98.3 5.3 %collective-permute-start.9 = (f32[128,128]{1,0:T(8,128)S(1)}, f32[128,128]{1,0:T(8,128)S(1)}, u32[]{:S(2)}, u32[]{:S(2)}) collective-permute-start(f32[128,128]{1,0:T(8,128)S(1)} %get-tuple-element.37), channel_id=1, source_target_pairs={{0,4},{4,0},{1,5},{5,1},{2,6},{6,2},{3,7},{7,3},{8,12},{12,8},{9,1... | collective-permute-start | bytes 196616 | tf_op jit(solution)/shard_map/ppermute | solution.py:33
